TPU v7x, 32 devices: a whole 2x2x4 slice. The times are simulated.
32 devices in a mesh: brow: 4 (over y, x), bcol: 8 (over z, core).
Axes of the slice: x: 2, y: 2, z: 4, core: 2. Of those that a mesh axis runs over, the one named last changes fastest.
Arguments:
- panel_points: bfloat16 [3, 6144], P(None, ('brow', 'bcol')), may hold values from 0 to 1
- panel_map: int32 [3, 6144], replicated, may hold values from 0 to 2047, as said below
- element_nodes: int32 [125, 1024], P(None, ('brow', 'bcol')), may hold values from 0 to 2047
- element_coef: float32 [1024], P(('brow', 'bcol')), may hold values from 0.1 to 1
- element_matrix: float32 [125, 125], replicated, as said below
- node_mass: float32 [65536], P(('brow', 'bcol')), may hold values from 2 to 4
- forcing: float32 [64, 65536], P(None, ('brow', 'bcol')), may hold values from -6 to 6
- field_start: float32 [64, 65536], P(None, ('brow', 'bcol')), may hold values from -6 to 6
- potential_start: float32 [64, 6144], P(None, ('brow', 'bcol')), may hold values from -6 to 6
Outputs:
- fem_field: float32 [64, 65536], P(None, ('brow', 'bcol'))
- potential: float32 [64, 6144], P(None, ('brow', 'bcol'))
Inputs may be any that keep to these rules, and one draw needn't show every extreme that they name: `panel_map`: row 0 is an index over brow+bcol (brow slowest), row 2 a local node below 2048. In each aligned block of 192 panels every group owns either no panel or exactly 12 of them, whose row 1 values are 0 to 11, each once. `element_nodes`: local node numbers within the element's own group. `element_matrix`: Symmetric.
All inputs are finite; a program needn't handle non-finite values.
Results may differ from a plain program's by a relative error of at most 0.0015.
The roundings to bfloat16 on the way count: a program that leaves them out, or rounds other values in their place, can miss the bound.
Values may be sent and summed in bfloat16 or wider, within the bound.
No kernel may reach another device: no remote copies, remote signals or barrier semaphores. Data moves between devices by JAX's collectives and lax.ppermute only.
A program may use at most 128 MiB of HBM per device.

v0:
```python
import math

import jax
import jax.numpy as jnp
from jax import lax
from jax.sharding import PartitionSpec as P

RIM = 128
SWEEPS = 3
ITERS = 2


wave_number = 20.0
penalty = 0.5


def padded_2(block, sides, width):
    for axis, dim in sides:
        count = lax.axis_size(axis)
        forward = [(i, i + 1) for i in range(count - 1)]
        backward = [(target, source) for source, target in forward]
        low = lax.ppermute(
            lax.slice_in_dim(block, block.shape[dim] - width, None, axis=dim), axis, forward
        )
        high = lax.ppermute(lax.slice_in_dim(block, 0, width, axis=dim), axis, backward)
        block = jnp.concatenate([low, block, high], axis=dim)
    return block


def kernel_pair(sources, targets, count_all):
    src_xyz = sources.astype(jnp.float32)
    tgt_xyz = targets.astype(jnp.float32)
    delta_xyz = src_xyz[:, :, None] - tgt_xyz[:, None, :]
    dist_sq = jnp.sum(delta_xyz * delta_xyz, axis=0)
    soften = 0.5 * float(count_all) ** (-1.0 / 3.0)
    radius = jnp.sqrt(dist_sq + soften * soften)
    scaling = 1.0 / (radius * math.sqrt(float(count_all)))
    real_tile = (jnp.cos(wave_number * radius) * scaling).astype(jnp.bfloat16)
    imag_tile = (jnp.sin(wave_number * radius) * scaling).astype(jnp.bfloat16)
    return (real_tile, imag_tile)


def apply_tiles(running, densities, real_tile, imag_tile):
    half_rows = densities.shape[0] // 2
    turned = jnp.concatenate([-densities[half_rows:], densities[:half_rows]], axis=0)
    first = jnp.dot(densities, real_tile, preferred_element_type=jnp.float32)
    second = jnp.dot(turned, imag_tile, preferred_element_type=jnp.float32)
    return running + first + second


def make_build(targets, count_all):

    def build(state_now, shard_piece, offset):
        densities, sources = shard_piece
        span_rows = densities.shape[1]
        block_rows = 512

        def one_block(state_in, block_index):
            running, store_real, store_imag = state_in
            block_start = block_index * block_rows
            dense_part = lax.dynamic_slice_in_dim(densities, block_start, block_rows, 1)
            source_part = lax.dynamic_slice_in_dim(sources, block_start, block_rows, 1)
            real_tile, imag_tile = kernel_pair(source_part, targets, count_all)
            running = apply_tiles(running, dense_part, real_tile, imag_tile)
            store_real = lax.dynamic_update_slice_in_dim(store_real, real_tile, block_start, 0)
            store_imag = lax.dynamic_update_slice_in_dim(store_imag, imag_tile, block_start, 0)
            return ((running, store_real, store_imag), None)

        state_out, unused = lax.scan(
            one_block, state_now, jnp.arange(span_rows // block_rows, dtype=jnp.int32)
        )
        return state_out

    return build


def make_reuse(store_real, store_imag):

    def reuse(running, densities, offset):
        return apply_tiles(running, densities, store_real, store_imag)

    return reuse


def apply_operator(field_now, element_nodes, element_coef, element_matrix, node_mass):
    padded = padded_2(field_now.astype(jnp.bfloat16), ((("brow", "bcol"), 1),), RIM).astype(
        field_now.dtype
    )
    from_left = padded[:, :RIM]
    from_right = padded[:, padded.shape[1] - RIM :]
    gathered = jnp.take(field_now, element_nodes, axis=1)
    stiffness = (
        jnp.einsum("jk,cke->cje", element_matrix, gathered, precision=lax.Precision.HIGHEST)
        * element_coef
    )
    result = node_mass * field_now + jnp.zeros_like(field_now).at[:, element_nodes].add(stiffness)
    result = result.at[:, :RIM].add(-penalty * from_left)
    result = result.at[:, result.shape[1] - RIM :].add(-penalty * from_right)
    return result


def per_device(
    panel_points,
    panel_map,
    element_nodes,
    element_coef,
    element_matrix,
    node_mass,
    forcing,
    field_start,
    potential_start,
):
    columns, panel_dev = potential_start.shape
    devices = lax.axis_size("brow") * lax.axis_size("bcol")
    count_all = panel_dev * devices
    capacity = max(2, 2 * panel_dev // devices)
    self_rank = lax.axis_index("brow") * lax.axis_size("bcol") + lax.axis_index("bcol")
    panel_owner = panel_map[0]
    panel_slot = panel_map[1]
    local_node = panel_map[2]
    panel_block = jnp.arange(count_all, dtype=jnp.int32) // panel_dev
    slot_total = devices * capacity
    table_index = jnp.where(
        panel_owner == self_rank, panel_block * capacity + panel_slot, slot_total
    )
    node_table = jnp.zeros((slot_total,), jnp.int32).at[table_index].set(local_node, mode="drop")
    own_owner = lax.dynamic_slice_in_dim(panel_owner, self_rank * panel_dev, panel_dev)
    own_slot = lax.dynamic_slice_in_dim(panel_slot, self_rank * panel_dev, panel_dev)
    local_index = own_owner * capacity + own_slot
    targets = lax.all_gather(panel_points, "brow", axis=1, tiled=True)
    source_rows = panel_dev * lax.axis_size("bcol")
    store_real = jnp.zeros((source_rows, targets.shape[1]), jnp.bfloat16)
    store_imag = jnp.zeros((source_rows, targets.shape[1]), jnp.bfloat16)
    build = make_build(targets, count_all)
    field_now = field_start
    potential_now = potential_start
    for turn_index in range(ITERS):
        trace_out = jnp.take(field_now, node_table, axis=1).astype(jnp.bfloat16)
        load_out = (
            jnp.zeros((columns, slot_total), jnp.bfloat16)
            .at[:, local_index]
            .set(potential_now.astype(jnp.bfloat16))
        )
        trace_in, load_in = (
            lax.all_to_all(trace_out, ("brow", "bcol"), split_axis=1, concat_axis=1, tiled=True),
            lax.all_to_all(load_out, ("brow", "bcol"), split_axis=1, concat_axis=1, tiled=True),
        )
        densities = jnp.take(trace_in, local_index, axis=1)
        rhs = forcing + jnp.zeros_like(forcing).at[:, node_table].add(load_in.astype(jnp.float32))
        new_field = field_now
        for sweep in range(SWEEPS):
            weight = 1.0 / (1.25 + 0.75 * math.cos(math.pi * (2 * sweep + 1) / (2.0 * SWEEPS)))
            residual = rhs - apply_operator(
                new_field, element_nodes, element_coef, element_matrix, node_mass
            )
            new_field = new_field + weight * residual / node_mass
        running = jnp.zeros((columns, targets.shape[1]), jnp.float32)
        if turn_index == 0:
            state_init = (running, store_real, store_imag)
            running, store_real, store_imag = build(
                state_init,
                (
                    lax.all_gather(densities, "bcol", axis=1, tiled=True),
                    lax.all_gather(panel_points, "bcol", axis=1, tiled=True),
                ),
                jnp.int32(0),
            )
        else:
            reuse = make_reuse(store_real, store_imag)
            running = reuse(
                running, lax.all_gather(densities, "bcol", axis=1, tiled=True), jnp.int32(0)
            )
        new_potential = lax.psum_scatter(running, "brow", scatter_dimension=1, tiled=True)
        field_now = new_field
        potential_now = new_potential
    return (field_now, potential_now)


def solution(mesh):
    placed = (
        P(None, ("brow", "bcol")),
        P(),
        P(None, ("brow", "bcol")),
        P(("brow", "bcol")),
        P(),
        P(("brow", "bcol")),
        P(None, ("brow", "bcol")),
        P(None, ("brow", "bcol")),
        P(None, ("brow", "bcol")),
    )
    return jax.shard_map(
        per_device,
        mesh=mesh,
        in_specs=placed,
        out_specs=(P(None, ("brow", "bcol")), P(None, ("brow", "bcol"))),
        check_vma=False,
    )
```

profile of v0, /device:TPU:4, one launch (start us, length us, event | category | flops | bytes accessed | tf_op | source)
XLA Modules:
  0.0 588.6 jit_solution(2023458437762007259)
XLA Ops:
  12.2 7.2 %collective-permute-start.1 = (bf16[64,128]{0,1:T(8,128)(2,1)}, bf16[64,128]{0,1:T(8,128)(2,1)}, u32[]{:S(2)}, u32[]{:S(2)}) collective-permute-start(bf16[64,128]{0,1:T(8,128)(2,1)} %get-tuple-element.282), channel_id=1, source_target_pairs={{1,0},{2,1},{3,2},{4,3},{5,4},{6,5},{7,6},{8,7},{9,8},{10,9},{11,1... | collective-permute-start | bytes 49160 | tf_op jit(solution)/shard_map/ppermute | solution.py:25
  22.2 2.5 all-to-all-start
  24.9 23.0 %scatter_custom_fusion = s32[384]{0:T(512)S(1)} fusion(s32[6144]{0:T(1024)S(1)} %bitcast.179, s32[6144]{0:T(1024)S(1)} %bitcast.178, s32[]{:T(128)} %constant.341.clone.1), kind=kCustom, calls=%fused_computation.177 | custom fusion | bytes 1540 | tf_op jit(solution)/shard_map/scatter | solution.py:126
  49.1 14.1 %gather_fusion = f32[4000,64]{1,0:T(8,128)} fusion(f32[64,2048]{0,1:T(8,128)S(1)} %copy.137, s32[4096]{0:T(1024)S(1)} %pad_clamp_fusion), kind=kCustom, calls=%fused_computation.clone | custom fusion | bytes 2064000 | tf_op jit(solution)/shard_map/jit(_take)/gather | solution.py:91
  63.2 3.7 copy.134
  66.9 3.2 fusion.11
  70.7 4.0 copy.135
  76.1 2.3 copy.191
  80.0 12.7 %all-gather.1 = bf16[8,192,3]{1,2,0:T(4,128)(2,1)S(1)} all-gather(bf16[1,192,3]{1,2,0:T(4,128)(2,1)S(1)} %bitcast.180), channel_id=1, replica_groups=mesh['brow'=4,'bcol'=8] {'bcol'}, dimensions={0}, use_global_device_ids=true | all-gather | bytes 10368 | tf_op jit(solution)/shard_map/all_gather | solution.py:164
  93.4 8.0 %all-gather.2 = bf16[4,192,3]{1,2,0:T(4,128)(2,1)S(1)} all-gather(bf16[1,192,3]{1,2,0:T(4,128)(2,1)S(1)} %bitcast.181), channel_id=1, replica_groups=mesh['brow'=4,'bcol'=8] {'brow'}, dimensions={0}, use_global_device_ids=true | all-gather | bytes 5760 | tf_op jit(solution)/shard_map/all_gather | solution.py:130
  101.5 23.1 %scatter_fusion = f32[64,2048]{0,1:T(8,128)S(1)} fusion(f32[64,2048]{0,1:T(8,128)S(1)} %get-tuple-element.270, s32[4000]{0:T(1024)S(1)} %reshape.534, f32[4000,64]{1,0:T(8,128)} %bitcast.155), kind=kCustom, calls=%fused_computation.13 | custom fusion | flops 256000 | bytes 3088000 | tf_op jit(solution)/shard_map/scatter-add | solution.py:96
  126.9 5.2 scatter_custom_fusion.2
  132.1 2.4 fusion.82
  134.5 14.1 %gather_fusion.1 = f32[4000,64]{1,0:T(8,128)} fusion(f32[64,2048]{0,1:T(8,128)S(1)} %get-tuple-element.262, s32[4096]{0:T(1024)S(1)} %pad_clamp_fusion), kind=kCustom, calls=%fused_computation.3.clone | custom fusion | bytes 2064000 | tf_op jit(solution)/shard_map/jit(_take)/gather | solution.py:91
  149.0 3.7 copy.139
  152.7 1.9 collective-permute-start.2
  154.6 7.2 %collective-permute-start.3 = (bf16[64,128]{0,1:T(8,128)(2,1)S(1)}, bf16[64,128]{0,1:T(8,128)(2,1)S(1)}, u32[]{:S(2)}, u32[]{:S(2)}) collective-permute-start(bf16[64,128]{0,1:T(8,128)(2,1)S(1)} %get-tuple-element.280), channel_id=1, source_target_pairs={{1,0},{2,1},{3,2},{4,3},{5,4},{6,5},{7,6},{8,7},{9,8},{10,9},{11,1... | collective-permute-start | bytes 49160 | tf_op jit(solution)/shard_map/ppermute | solution.py:25
  161.8 3.2 fusion.10
  165.1 4.0 copy.140
  169.1 23.1 %scatter_fusion.1 = f32[64,2048]{0,1:T(8,128)S(1)} fusion(f32[64,2048]{0,1:T(8,128)S(1)} %broadcast_multiply_fusion.4, s32[4000]{0:T(1024)S(1)} %reshape.534, f32[4000,64]{1,0:T(8,128)} %bitcast.158), kind=kCustom, calls=%fused_computation.14 | custom fusion | flops 256000 | bytes 3088000 | tf_op jit(solution)/shard_map/scatter-add | solution.py:96
  192.9 2.4 fusion.81
  195.3 14.1 %gather_fusion.2 = f32[4000,64]{1,0:T(8,128)} fusion(f32[64,2048]{0,1:T(8,128)S(1)} %get-tuple-element.260, s32[4096]{0:T(1024)S(1)} %pad_clamp_fusion), kind=kCustom, calls=%fused_computation.4.clone | custom fusion | bytes 2064000 | tf_op jit(solution)/shard_map/jit(_take)/gather | solution.py:91
  209.7 3.7 copy.142
  213.4 1.9 collective-permute-start.4
  215.4 7.2 %collective-permute-start.5 = (bf16[64,128]{0,1:T(8,128)(2,1)S(1)}, bf16[64,128]{0,1:T(8,128)(2,1)S(1)}, u32[]{:S(2)}, u32[]{:S(2)}) collective-permute-start(bf16[64,128]{0,1:T(8,128)(2,1)S(1)} %get-tuple-element.278), channel_id=1, source_target_pairs={{1,0},{2,1},{3,2},{4,3},{5,4},{6,5},{7,6},{8,7},{9,8},{10,9},{11,1... | collective-permute-start | bytes 49160 | tf_op jit(solution)/shard_map/ppermute | solution.py:25
  222.6 3.2 fusion.9
  225.8 4.0 copy.143
  229.9 23.3 %scatter_fusion.2 = f32[64,2048]{0,1:T(8,128)S(1)} fusion(f32[64,2048]{0,1:T(8,128)S(1)} %broadcast_multiply_fusion.3, s32[4000]{0:T(1024)S(1)} %reshape.534, f32[4000,64]{1,0:T(8,128)} %bitcast.159), kind=kCustom, calls=%fused_computation.15 | custom fusion | flops 256000 | bytes 3088000 | tf_op jit(solution)/shard_map/scatter-add | solution.py:96
  253.9 2.4 fusion.80
  257.4 14.1 %gather_fusion.5 = f32[4000,64]{1,0:T(8,128)} fusion(f32[64,2048]{0,1:T(8,128)S(1)} %get-tuple-element.258, s32[4096]{0:T(1024)S(1)} %pad_clamp_fusion), kind=kCustom, calls=%fused_computation.5.clone | custom fusion | bytes 2064000 | tf_op jit(solution)/shard_map/jit(_take)/gather | solution.py:91
  273.3 3.0 all-to-all-start.1
  276.3 3.7 copy.152
  280.0 2.2 fusion.8
  284.6 5.0 all-to-all-start.3
  291.1 2.8 copy.153
  293.9 2.0 collective-permute-start.6
  295.9 7.1 %collective-permute-start.7 = (bf16[64,128]{0,1:T(8,128)(2,1)}, bf16[64,128]{0,1:T(8,128)(2,1)}, u32[]{:S(2)}, u32[]{:S(2)}) collective-permute-start(bf16[64,128]{0,1:T(8,128)(2,1)} %get-tuple-element.276), channel_id=1, source_target_pairs={{1,0},{2,1},{3,2},{4,3},{5,4},{6,5},{7,6},{8,7},{9,8},{10,9},{11,1... | collective-permute-start | bytes 49160 | tf_op jit(solution)/shard_map/ppermute | solution.py:25
  303.0 23.1 %scatter_fusion.3 = f32[64,2048]{0,1:T(8,128)S(1)} fusion(f32[64,2048]{0,1:T(8,128)S(1)} %broadcast_multiply_fusion.2, s32[4000]{0:T(1024)S(1)} %reshape.534, f32[4000,64]{1,0:T(8,128)} %bitcast.156), kind=kCustom, calls=%fused_computation.18 | custom fusion | flops 256000 | bytes 3088000 | tf_op jit(solution)/shard_map/scatter-add | solution.py:96
  329.1 14.4 %all-gather = bf16[8,192,64]{1,2,0:T(8,128)(2,1)S(1)} all-gather(bf16[1,192,64]{1,2,0:T(8,128)(2,1)S(1)} %copy.145), channel_id=1, replica_groups=mesh['brow'=4,'bcol'=8] {'bcol'}, dimensions={0}, use_global_device_ids=true | all-gather | bytes 221184 | tf_op jit(solution)/shard_map/all_gather | solution.py:163
  347.8 37.6 %while.27 = (s32[]{:T(128)}, f32[64,768]{1,0:T(8,128)S(1)}, bf16[1536,768]{1,0:T(8,128)(2,1)}, bf16[1536,768]{1,0:T(8,128)(2,1)}, s32[3]{0:T(128)S(1)}, /*index=...) while((s32[]{:T(128)}, f32[64,768]{1,0:T(8,128)S(1)}, ...), condition=%wide.region_9.13_spmd.clone, body=%wide.region_7.12_spmd.clone.sunk | while | flops 107286280 | bytes 8951521 | solution.py:69
  350.2 7.6 %constant_dynamic-update-slice_fusion.3 = (bf16[1536,768]{1,0:T(8,128)(2,1)}, bf16[512,768]{1,0:T(8,128)(2,1)S(1)}, bf16[1536,768]{1,0:T(8,128)(2,1)}, bf16[512,768]{1,0:T(8,128)(2,1)}) fusion(bf16[1536,768]{1,0:T(8,128)(2,1)} %get-tuple-element.369, s32[]{:T(128)S(6)} %select_n.191, f32[512,768]{1,0:T(8,128)S(1)} %multiply_reduce_fusion.2, ...), kind=kLoop, calls=%fused_computation.35.clone.1 | loop fusion | flops 3145728 | bytes 4718596 | tf_op jit(solution)/shard_map/while/body/eval_jaxpr/dynamic_update_slice | solution.py:66
  362.8 7.6 %constant_dynamic-update-slice_fusion.3 = (bf16[1536,768]{1,0:T(8,128)(2,1)}, bf16[512,768]{1,0:T(8,128)(2,1)S(1)}, bf16[1536,768]{1,0:T(8,128)(2,1)}, bf16[512,768]{1,0:T(8,128)(2,1)}) fusion(bf16[1536,768]{1,0:T(8,128)(2,1)} %get-tuple-element.369, s32[]{:T(128)S(6)} %select_n.191, f32[512,768]{1,0:T(8,128)S(1)} %multiply_reduce_fusion.2, ...), kind=kLoop, calls=%fused_computation.35.clone.1 | loop fusion | flops 3145728 | bytes 4718596 | tf_op jit(solution)/shard_map/while/body/eval_jaxpr/dynamic_update_slice | solution.py:66
  375.3 7.6 %constant_dynamic-update-slice_fusion.3 = (bf16[1536,768]{1,0:T(8,128)(2,1)}, bf16[512,768]{1,0:T(8,128)(2,1)S(1)}, bf16[1536,768]{1,0:T(8,128)(2,1)}, bf16[512,768]{1,0:T(8,128)(2,1)}) fusion(bf16[1536,768]{1,0:T(8,128)(2,1)} %get-tuple-element.369, s32[]{:T(128)S(6)} %select_n.191, f32[512,768]{1,0:T(8,128)S(1)} %multiply_reduce_fusion.2, ...), kind=kLoop, calls=%fused_computation.35.clone.1 | loop fusion | flops 3145728 | bytes 4718596 | tf_op jit(solution)/shard_map/while/body/eval_jaxpr/dynamic_update_slice | solution.py:66
  385.5 14.2 %all-gather.3 = bf16[8,192,64]{1,2,0:T(8,128)(2,1)S(1)} all-gather(bf16[1,192,64]{1,2,0:T(8,128)(2,1)S(1)} %copy.160), channel_id=1, replica_groups=mesh['brow'=4,'bcol'=8] {'bcol'}, dimensions={0}, use_global_device_ids=true | all-gather | bytes 221184 | tf_op jit(solution)/shard_map/all_gather | solution.py:171
  401.1 2.3 fusion.92
  406.4 16.6 %reduce-scatter.7.cloned.1.call-done = f32[192,64]{1,0:T(8,128)} async-done(((f32[768,64]{1,0:T(8,128)}), f32[192,64]{1,0:T(8,128)}) %reduce-scatter.7.cloned.1.call-update) | async-done | bytes 49168
  426.2 4.9 all-to-all-start.2
  431.9 18.4 %reduce-scatter.9.cloned.1.call-done = f32[192,64]{1,0:T(8,128)} async-done(((f32[768,64]{1,0:T(8,128)}), f32[192,64]{1,0:T(8,128)}) %reduce-scatter.9.cloned.1.call-update) | async-done | bytes 49168
  452.1 4.8 scatter_custom_fusion.7
  456.8 2.4 fusion.79
  459.2 14.1 %gather_fusion.6 = f32[4000,64]{1,0:T(8,128)} fusion(f32[64,2048]{0,1:T(8,128)S(1)} %get-tuple-element.256, s32[4096]{0:T(1024)S(1)} %pad_clamp_fusion), kind=kCustom, calls=%fused_computation.6.clone | custom fusion | bytes 2064000 | tf_op jit(solution)/shard_map/jit(_take)/gather | solution.py:91
  473.7 3.7 copy.155
  477.4 1.9 collective-permute-start.8
  479.3 7.2 %collective-permute-start.9 = (bf16[64,128]{0,1:T(8,128)(2,1)S(1)}, bf16[64,128]{0,1:T(8,128)(2,1)S(1)}, u32[]{:S(2)}, u32[]{:S(2)}) collective-permute-start(bf16[64,128]{0,1:T(8,128)(2,1)S(1)} %get-tuple-element.274), channel_id=1, source_target_pairs={{1,0},{2,1},{3,2},{4,3},{5,4},{6,5},{7,6},{8,7},{9,8},{10,9},{11,1... | collective-permute-start | bytes 49160 | tf_op jit(solution)/shard_map/ppermute | solution.py:25
  486.6 3.2 fusion.7
  489.8 4.0 copy.156
  493.8 23.4 %scatter_fusion.4 = f32[64,2048]{0,1:T(8,128)S(1)} fusion(f32[64,2048]{0,1:T(8,128)S(1)} %broadcast_multiply_fusion.1, s32[4000]{0:T(1024)S(1)} %reshape.534, f32[4000,64]{1,0:T(8,128)} %bitcast.160), kind=kCustom, calls=%fused_computation.19 | custom fusion | flops 256000 | bytes 3088000 | tf_op jit(solution)/shard_map/scatter-add | solution.py:96
  517.9 2.4 fusion.78
  520.2 14.1 %gather_fusion.7 = f32[4000,64]{1,0:T(8,128)} fusion(f32[64,2048]{0,1:T(8,128)S(1)} %get-tuple-element.254, s32[4096]{0:T(1024)S(1)} %pad_clamp_fusion), kind=kCustom, calls=%fused_computation.7.clone | custom fusion | bytes 2064000 | tf_op jit(solution)/shard_map/jit(_take)/gather | solution.py:91
  534.7 3.7 copy.158
  540.4 7.2 %collective-permute-start.11 = (bf16[64,128]{0,1:T(8,128)(2,1)S(1)}, bf16[64,128]{0,1:T(8,128)(2,1)S(1)}, u32[]{:S(2)}, u32[]{:S(2)}) collective-permute-start(bf16[64,128]{0,1:T(8,128)(2,1)S(1)} %get-tuple-element.272), channel_id=1, source_target_pairs={{1,0},{2,1},{3,2},{4,3},{5,4},{6,5},{7,6},{8,7},{9,8},{10,9},{11,1... | collective-permute-start | bytes 49160 | tf_op jit(solution)/shard_map/ppermute | solution.py:25
  547.6 3.2 fusion.6
  550.8 4.0 copy.159
  554.8 23.1 %scatter_fusion.5 = f32[64,2048]{0,1:T(8,128)S(1)} fusion(f32[64,2048]{0,1:T(8,128)S(1)} %broadcast_multiply_fusion, s32[4000]{0:T(1024)S(1)} %reshape.534, f32[4000,64]{1,0:T(8,128)} %bitcast.157), kind=kCustom, calls=%fused_computation.20 | custom fusion | flops 256000 | bytes 3088000 | tf_op jit(solution)/shard_map/scatter-add | solution.py:96
  (183 shorter events, 60.9 us)
Async XLA Ops:
  7.2 59.7 %copy-start = (f32[125,125]{1,0:T(8,128)S(1)}, f32[125,125]{1,0:T(8,128)}, u32[]{:S(2)}) copy-start(f32[125,125]{1,0:T(8,128)} %param.45) | copy-start | bytes 187504
  7.2 12.3 %copy-start.12 = (s32[3,6144]{1,0:T(4,128)S(1)}, s32[3,6144]{1,0:T(4,128)}, u32[]{:S(2)}) copy-start(s32[3,6144]{1,0:T(4,128)} %param.42) | copy-start | bytes 221188
  7.2 12.4 %copy-start.13 = (f32[64,192]{1,0:T(8,128)S(1)}, f32[64,192]{1,0:T(8,128)}, u32[]{:S(2)}) copy-start(f32[64,192]{1,0:T(8,128)} %param.49) | copy-start | bytes 147460
  8.6 16.1 %copy-start.14 = (s32[125,32]{0,1:T(8,128)S(1)}, s32[125,32]{0,1:T(8,128)}, u32[]{:S(2)}) copy-start(s32[125,32]{0,1:T(8,128)} %param.43) | copy-start | bytes 48004
  10.3 115.0 %collective-permute-start = (bf16[64,128]{0,1:T(8,128)(2,1)}, bf16[64,128]{0,1:T(8,128)(2,1)S(1)}, u32[]{:S(2)}, u32[]{:S(2)}) collective-permute-start(bf16[64,128]{0,1:T(8,128)(2,1)} %get-tuple-element.281), channel_id=1, source_target_pairs={{0,1},{1,2},{2,3},{3,4},{4,5},{5,6},{6,7},{7,8},{8,9},{9,10},{10,1... | collective-permute-start | bytes 49160 | tf_op jit(solution)/shard_map/ppermute | solution.py:22
  12.2 113.1 %collective-permute-start.1 = (bf16[64,128]{0,1:T(8,128)(2,1)}, bf16[64,128]{0,1:T(8,128)(2,1)}, u32[]{:S(2)}, u32[]{:S(2)}) collective-permute-start(bf16[64,128]{0,1:T(8,128)(2,1)} %get-tuple-element.282), channel_id=1, source_target_pairs={{1,0},{2,1},{3,2},{4,3},{5,4},{6,5},{7,6},{8,7},{9,8},{10,9},{11,1... | collective-permute-start | bytes 49160 | tf_op jit(solution)/shard_map/ppermute | solution.py:25
  19.8 0.5 copy-start.23
  22.2 104.6 %all-to-all-start = ((bf16[32,2,384]{2,1,0:T(2,128)(2,1)}), bf16[32,2,384]{2,1,0:T(2,128)(2,1)S(1)}, u32[]{:S(2)}, u32[]{:S(2)}) async-start(bf16[32,2,384]{2,1,0:T(2,128)(2,1)} %reshape.681), calls=%async_computation | async-start | bytes 98304 | tf_op jit(solution)/shard_map/all_to_all | solution.py:146
  24.8 197.9 %copy-start.10 = (pred[125,32]{0,1:T(8,128)(4,1)}, pred[125,32]{0,1:T(8,128)(4,1)S(1)}, u32[]{:S(2)}) copy-start(pred[125,32]{0,1:T(8,128)(4,1)S(1)} %compare_and_fusion) | copy-start | bytes 12004
  47.8 19.0 %copy-start.21 = (s32[384]{0:T(512)}, s32[384]{0:T(512)S(1)}, u32[]{:S(2)}) copy-start(s32[384]{0:T(512)S(1)} %compare_select_fusion.3) | copy-start | bytes 4612
  63.2 3.7 copy-start.15
  66.9 11.5 %copy-start.17 = (s32[1024]{0:T(1024)}, s32[1024]{0:T(1024)S(1)}, u32[]{:S(2)}) copy-start(s32[1024]{0:T(1024)S(1)} %pad_clamp_fusion.2) | copy-start | bytes 12292
  70.1 4.6 copy-start.8
  74.7 5.3 copy-start.20
  124.7 7.5 %copy-start.7 = (f32[2048]{0:T(1024)S(1)}, f32[2048]{0:T(1024)}, u32[]{:S(2)}) copy-start(f32[2048]{0:T(1024)} %param.46) | copy-start | bytes 24580
  148.9 3.7 copy-start.4
  152.7 39.5 %collective-permute-start.2 = (bf16[64,128]{0,1:T(8,128)(2,1)S(1)}, bf16[64,128]{0,1:T(8,128)(2,1)S(1)}, u32[]{:S(2)}, u32[]{:S(2)}) collective-permute-start(bf16[64,128]{0,1:T(8,128)(2,1)S(1)} %get-tuple-element.279), channel_id=1, source_target_pairs={{0,1},{1,2},{2,3},{3,4},{4,5},{5,6},{6,7},{7,8},{8,9},{9,10},{10,1... | collective-permute-start | bytes 49160 | tf_op jit(solution)/shard_map/ppermute | solution.py:22
  154.6 37.6 %collective-permute-start.3 = (bf16[64,128]{0,1:T(8,128)(2,1)S(1)}, bf16[64,128]{0,1:T(8,128)(2,1)S(1)}, u32[]{:S(2)}, u32[]{:S(2)}) collective-permute-start(bf16[64,128]{0,1:T(8,128)(2,1)S(1)} %get-tuple-element.280), channel_id=1, source_target_pairs={{1,0},{2,1},{3,2},{4,3},{5,4},{6,5},{7,6},{8,7},{9,8},{10,9},{11,1... | collective-permute-start | bytes 49160 | tf_op jit(solution)/shard_map/ppermute | solution.py:25
  209.7 3.7 copy-start.5
  213.4 39.7 %collective-permute-start.4 = (bf16[64,128]{0,1:T(8,128)(2,1)S(1)}, bf16[64,128]{0,1:T(8,128)(2,1)S(1)}, u32[]{:S(2)}, u32[]{:S(2)}) collective-permute-start(bf16[64,128]{0,1:T(8,128)(2,1)S(1)} %get-tuple-element.277), channel_id=1, source_target_pairs={{0,1},{1,2},{2,3},{3,4},{4,5},{5,6},{6,7},{7,8},{8,9},{9,10},{10,1... | collective-permute-start | bytes 49160 | tf_op jit(solution)/shard_map/ppermute | solution.py:22
  215.4 37.8 %collective-permute-start.5 = (bf16[64,128]{0,1:T(8,128)(2,1)S(1)}, bf16[64,128]{0,1:T(8,128)(2,1)S(1)}, u32[]{:S(2)}, u32[]{:S(2)}) collective-permute-start(bf16[64,128]{0,1:T(8,128)(2,1)S(1)} %get-tuple-element.278), channel_id=1, source_target_pairs={{1,0},{2,1},{3,2},{4,3},{5,4},{6,5},{7,6},{8,7},{9,8},{10,9},{11,1... | collective-permute-start | bytes 49160 | tf_op jit(solution)/shard_map/ppermute | solution.py:25
  253.9 2.4 copy-start.18
  271.5 0.9 copy-start.9
  271.5 0.9 copy-start.22
  273.3 11.2 %all-to-all-start.1 = ((bf16[32,2,384]{2,1,0:T(2,128)(2,1)}), bf16[32,2,384]{2,1,0:T(2,128)(2,1)}, u32[]{:S(2)}, u32[]{:S(2)}) async-start(bf16[32,2,384]{2,1,0:T(2,128)(2,1)} %reshape.683), calls=%async_computation.1 | async-start | bytes 98304 | tf_op jit(solution)/shard_map/all_to_all | solution.py:145
  284.6 42.6 %all-to-all-start.3 = ((bf16[32,2,384]{2,1,0:T(2,128)(2,1)}), bf16[32,2,384]{2,1,0:T(2,128)(2,1)S(1)}, u32[]{:S(2)}, u32[]{:S(2)}) async-start(bf16[32,2,384]{2,1,0:T(2,128)(2,1)} %reshape.687), calls=%async_computation.3 | async-start | bytes 98304 | tf_op jit(solution)/shard_map/all_to_all | solution.py:145
  289.6 133.4 %reduce-scatter.7.cloned.1.call-start = ((), (), s32[]{:S(2)}) async-start(), calls=%async_computation.6 | async-start | bytes 491520
  293.9 111.1 %collective-permute-start.6 = (bf16[64,128]{0,1:T(8,128)(2,1)}, bf16[64,128]{0,1:T(8,128)(2,1)}, u32[]{:S(2)}, u32[]{:S(2)}) collective-permute-start(bf16[64,128]{0,1:T(8,128)(2,1)} %get-tuple-element.275), channel_id=1, source_target_pairs={{0,1},{1,2},{2,3},{3,4},{4,5},{5,6},{6,7},{7,8},{8,9},{9,10},{10,1... | collective-permute-start | bytes 49160 | tf_op jit(solution)/shard_map/ppermute | solution.py:22
  295.9 109.1 %collective-permute-start.7 = (bf16[64,128]{0,1:T(8,128)(2,1)}, bf16[64,128]{0,1:T(8,128)(2,1)}, u32[]{:S(2)}, u32[]{:S(2)}) collective-permute-start(bf16[64,128]{0,1:T(8,128)(2,1)} %get-tuple-element.276), channel_id=1, source_target_pairs={{1,0},{2,1},{3,2},{4,3},{5,4},{6,5},{7,6},{8,7},{9,8},{10,9},{11,1... | collective-permute-start | bytes 49160 | tf_op jit(solution)/shard_map/ppermute | solution.py:25
  303.0 24.3 %copy-start.19 = (s32[1024]{0:T(1024)S(1)}, s32[1024]{0:T(1024)}, u32[]{:S(2)}) copy-start(s32[1024]{0:T(1024)} %pad_clamp_fusion.1) | copy-start | bytes 12292
  303.0 25.9 %copy-start.24 = (pred[192]{0:T(512)(128)(4,1)S(1)}, pred[192]{0:T(512)(128)(4,1)}, u32[]{:S(2)}) copy-start(pred[192]{0:T(512)(128)(4,1)} %compare_and_fusion.1) | copy-start | bytes 580
  401.1 49.2 %reduce-scatter.9.cloned.1.call-start = ((), (), s32[]{:S(2)}) async-start(), calls=%async_computation.7 | async-start | bytes 491520
  401.1 2.4 copy-start.1
  403.5 1.5 copy-start.2
  426.2 25.7 %all-to-all-start.2 = ((bf16[32,2,384]{2,1,0:T(2,128)(2,1)}), bf16[32,2,384]{2,1,0:T(2,128)(2,1)S(1)}, u32[]{:S(2)}, u32[]{:S(2)}) async-start(bf16[32,2,384]{2,1,0:T(2,128)(2,1)} %reshape.685), calls=%async_computation.2 | async-start | bytes 98304 | tf_op jit(solution)/shard_map/all_to_all | solution.py:146
  473.6 3.8 copy-start.6
  473.6 12.9 %copy-start.11 = (pred[125,32]{0,1:T(8,128)(4,1)S(1)}, pred[125,32]{0,1:T(8,128)(4,1)}, u32[]{:S(2)}) copy-start(pred[125,32]{0,1:T(8,128)(4,1)} %copy-done.10) | copy-start | bytes 12004
  473.6 12.9 %copy-start.16 = (f32[32]{0:T(128)S(1)}, f32[32]{0:T(128)}, u32[]{:S(2)}) copy-start(f32[32]{0:T(128)} %param.44) | copy-start | bytes 388
  477.4 39.8 %collective-permute-start.8 = (bf16[64,128]{0,1:T(8,128)(2,1)S(1)}, bf16[64,128]{0,1:T(8,128)(2,1)S(1)}, u32[]{:S(2)}, u32[]{:S(2)}) collective-permute-start(bf16[64,128]{0,1:T(8,128)(2,1)S(1)} %get-tuple-element.273), channel_id=1, source_target_pairs={{0,1},{1,2},{2,3},{3,4},{4,5},{5,6},{6,7},{7,8},{8,9},{9,10},{10,1... | collective-permute-start | bytes 49160 | tf_op jit(solution)/shard_map/ppermute | solution.py:22
  479.3 37.9 %collective-permute-start.9 = (bf16[64,128]{0,1:T(8,128)(2,1)S(1)}, bf16[64,128]{0,1:T(8,128)(2,1)S(1)}, u32[]{:S(2)}, u32[]{:S(2)}) collective-permute-start(bf16[64,128]{0,1:T(8,128)(2,1)S(1)} %get-tuple-element.274), channel_id=1, source_target_pairs={{1,0},{2,1},{3,2},{4,3},{5,4},{6,5},{7,6},{8,7},{9,8},{10,9},{11,1... | collective-permute-start | bytes 49160 | tf_op jit(solution)/shard_map/ppermute | solution.py:25
  534.7 3.7 copy-start.3
  538.4 39.5 %collective-permute-start.10 = (bf16[64,128]{0,1:T(8,128)(2,1)S(1)}, bf16[64,128]{0,1:T(8,128)(2,1)S(1)}, u32[]{:S(2)}, u32[]{:S(2)}) collective-permute-start(bf16[64,128]{0,1:T(8,128)(2,1)S(1)} %get-tuple-element.271), channel_id=1, source_target_pairs={{0,1},{1,2},{2,3},{3,4},{4,5},{5,6},{6,7},{7,8},{8,9},{9,10},{10,1... | collective-permute-start | bytes 49160 | tf_op jit(solution)/shard_map/ppermute | solution.py:22
  540.4 37.6 %collective-permute-start.11 = (bf16[64,128]{0,1:T(8,128)(2,1)S(1)}, bf16[64,128]{0,1:T(8,128)(2,1)S(1)}, u32[]{:S(2)}, u32[]{:S(2)}) collective-permute-start(bf16[64,128]{0,1:T(8,128)(2,1)S(1)} %get-tuple-element.272), channel_id=1, source_target_pairs={{1,0},{2,1},{3,2},{4,3},{5,4},{6,5},{7,6},{8,7},{9,8},{10,9},{11,1... | collective-permute-start | bytes 49160 | tf_op jit(solution)/shard_map/ppermute | solution.py:25
Sparse Core Ops, SparseCore 0:
  401.2 21.7 reduce-scatter.6
  425.8 24.4 reduce-scatter.8
where the time goes:
time: 599 us; the launch traced here: 589 us
  other arithmetic  203 us (34%)
  local copies, waits for them, and re-layouts  187 us (31%)
  starting transfers between devices  70.5 us (12%)
  blocking collectives  49.4 us (8%)
  waiting for transfers between devices  35.1 us (6%)
  matrix products  26.2 us (4%)
  between operations  15.4 us (3%)
    scatter-add x6, other arithmetic, apply_operator(): jnp.zeros_like(field_now).at[:, element_nodes].add(stiffness)  139 us
    gather x12, local copies, waits for them, and re-layouts, apply_operator(): gathered = jnp.take(field_now, element_nodes, axis=1)  107 us
    ppermute x6, starting transfers between devices, padded_2(): lax.ppermute(lax.slice_in_dim(block, 0, width, axis=dim), axis, backward)  43.3 us
    unnamed x4, waiting for transfers between devices  35.1 us
    all_gather x2, blocking collectives, per_device(): lax.all_gather(densities, 'bcol', axis=1, tiled=True)  28.6 us
    mul x6, local copies, waits for them, and re-layouts, apply_operator(): jnp.einsum('jk,cke->cje', element_matrix, gathered, precision=lax.Precisi...  23 us
    scatter x1, local copies, waits for them, and re-layouts, per_device(): jnp.zeros((slot_total,), jnp.int32).at[table_index]  23 us
    dynamic_update_slice x3, other arithmetic, one_block(): lax.dynamic_update_slice_in_dim(store_imag, imag_tile, block_start, 0)  22.8 us
  transfers between devices with their start and end apart: 18, of which 2 were waited for; matrix products, arithmetic and copies ran while one was open for 50% of the time, Pallas kernels for 0%

commit v1 on v0

v1 whole, which is shorter than its diff:
```python
import functools
import math

import jax
import jax.numpy as jnp
from jax import lax
from jax.experimental import pallas as pl
from jax.experimental.pallas import tpu as pltpu
from jax.sharding import PartitionSpec as P

RIM = 128
SWEEPS = 3
LANES = 128
SLOT_ROWS = 8
HALVES = 2

wave_number = 20.0
penalty = 0.5

AXES = ("brow", "bcol")
F32 = jnp.float32
BF16 = jnp.bfloat16

SIN_POLY = (3.14159264, -5.16771008, 2.55007752, -0.59829129, 0.07765766)
COS_POLY = (0.99999995, -4.93479283, 4.05841135, -1.33187657, 0.21968961)

VMEM_LIMIT = 56 * 1024 * 1024


def weight_of(sweep):
    return 1.0 / (1.25 + 0.75 * math.cos(math.pi * (2 * sweep + 1) / (2.0 * SWEEPS)))


def call(kernel, out_shape, cost, **more):
    return pl.pallas_call(
        kernel,
        out_shape=out_shape,
        compiler_params=pltpu.CompilerParams(vmem_limit_bytes=VMEM_LIMIT),
        cost_estimate=pl.CostEstimate(flops=cost, bytes_accessed=1 << 20, transcendentals=0),
        **more,
    )


def shape_of(shape, dtype):
    return jax.ShapeDtypeStruct(shape, dtype)


def dot(a, b):
    return jnp.dot(a, b, preferred_element_type=F32)


def dot_nt(a, b):
    return lax.dot_general(a, b, (((1,), (1,)), ((), ())), preferred_element_type=F32)


def split_two(value):
    high = value.astype(BF16)
    return high, (value - high.astype(F32)).astype(BF16)


def low_part(value, size):
    return value & (size - 1) if size & (size - 1) == 0 else value % size


def high_part(value, size):
    return value >> (size.bit_length() - 1) if size & (size - 1) == 0 else value // size


def stack_parts(value, parts):
    width = value.shape[1] // parts
    return jnp.concatenate([value[:, i * width : (i + 1) * width] for i in range(parts)], axis=0)


def one_hot_rows(key, rows):
    seen = lax.broadcasted_iota(jnp.int32, (rows, key.shape[1]), 0)
    return jnp.where(seen == key, 1.0, 0.0).astype(BF16)


def pick_part(stacked, part, parts):
    rows = stacked.shape[0] // parts
    picked = stacked[(parts - 1) * rows :]
    for i in reversed(range(parts - 1)):
        picked = jnp.where(part == i, stacked[i * rows : (i + 1) * rows], picked)
    return picked


def gather_nodes(field, nodes, parts):
    width = field.shape[1] // parts
    hot = one_hot_rows(jnp.where(nodes < 0, -1, low_part(nodes, width)), width)
    found = dot(stack_parts(field.astype(BF16), parts), hot)
    return pick_part(found, high_part(nodes, width), parts)


def scatter_nodes(values, nodes, parts, count):
    width = count // parts
    hot = one_hot_rows(jnp.where(nodes < 0, -1, low_part(nodes, width)), width)
    masked = jnp.concatenate(
        [jnp.where(high_part(nodes, width) == i, values, 0.0) for i in range(parts)], axis=0
    ).astype(BF16)
    added = dot_nt(masked, hot)
    rows = values.shape[0]
    return jnp.concatenate([added[i * rows : (i + 1) * rows] for i in range(parts)], axis=1)


def trace_rows(field, nodes, parts, brow):
    found = gather_nodes(field, nodes, parts)
    turned = jnp.transpose(found)
    span = turned.shape[0] // (HALVES * brow)
    pieces = []
    for r in range(brow):
        base = r * HALVES * span
        pieces.append(
            jnp.concatenate(
                [turned[base : base + span], turned[base + span : base + HALVES * span]], axis=1
            ).astype(BF16)
        )
    return pieces


def load_rows(potential, own_map, devices):
    owner, slot = own_map[0:1], own_map[1:2]
    half_rows = devices * SLOT_ROWS
    key = high_part(slot, SLOT_ROWS) * half_rows + owner * SLOT_ROWS + low_part(slot, SLOT_ROWS)
    rows = dot_nt(one_hot_rows(key, HALVES * half_rows), potential.astype(BF16))
    return jnp.concatenate([rows[:half_rows], rows[half_rows:]], axis=1)


def setup_kernel(
    parts, brow, bcol, panel_dev, rank_ref, map_ref, own_ref, field_ref, potential_ref, points_ref,
    nodes_ref, small_ref, trace_ref, rim_low_ref, rim_high_ref,
):
    rank = rank_ref[0]
    devices = brow * bcol
    row_panels = bcol * panel_dev
    row_slots = HALVES * bcol * SLOT_ROWS
    lane = lax.broadcasted_iota(jnp.int32, (1, row_panels), 1).astype(F32)
    block = jnp.floor((lane + 0.5) * (1.0 / panel_dev)).astype(jnp.int32)
    row_id = lax.broadcasted_iota(jnp.int32, (8, row_panels), 0)
    tables = []
    for r in range(brow):
        span = slice(r * row_panels, (r + 1) * row_panels)
        owner, slot, node = map_ref[0:1, span], map_ref[1:2, span], map_ref[2:3, span]
        key = high_part(slot, SLOT_ROWS) * (bcol * SLOT_ROWS) + block * SLOT_ROWS + low_part(slot, SLOT_ROWS)
        key = jnp.where(owner == rank, key, -1)
        hot = one_hot_rows(key, row_slots)
        values = jnp.where(
            row_id == 0, high_part(node, 256), jnp.where(row_id == 1, low_part(node, 256), 1)
        ).astype(F32).astype(BF16)
        found = dot_nt(values, hot)
        table = jnp.where(found[2:3] > 0.5, found[0:1] * 256.0 + found[1:2], -1.0)
        tables.append(table.astype(jnp.int32))
    nodes = jnp.concatenate(tables, axis=1)
    nodes_ref[...] = jnp.broadcast_to(nodes, nodes_ref.shape)
    field = field_ref[...]
    rim_low_ref[...] = field[:, :RIM].astype(BF16)
    rim_high_ref[...] = field[:, field.shape[1] - RIM :].astype(BF16)
    loads = load_rows(potential_ref[...], own_ref[...], devices)
    loads = loads.reshape(devices, SLOT_ROWS, LANES)
    points = jnp.broadcast_to(points_ref[...].astype(F32)[None], (devices, 8, LANES))
    small_ref[...] = jnp.concatenate([loads, points], axis=1).astype(BF16)
    write_traces(trace_rows(field, nodes, parts, brow), trace_ref, bcol)


def write_traces(pieces, trace_ref, bcol):
    for r, piece in enumerate(pieces):
        for c in range(bcol):
            trace_ref[r * bcol + c] = piece


def rim_correction(value, left_ref, right_ref, mass, weight):
    step = weight * penalty
    low = value[:, :RIM] + step * left_ref[...].astype(F32) / mass[:, :RIM]
    last = value.shape[1] - RIM
    high = value[:, last:] + step * right_ref[...].astype(F32) / mass[:, last:]
    return jnp.concatenate([low, value[:, RIM:last], high], axis=1)


def sweep_kernel(
    parts, weight, weight_before, group, coef_ref, field_ref, rhs_ref, mass_ref, keys_ref, matrix_ref,
    *more_refs,
):
    if weight_before is not None:
        left_ref, right_ref, *more_refs = more_refs
    (
        out_ref, field_scr, high_ref, low_ref, hot_ref, found_ref, local_ref, yhigh_ref, ylow_ref, sum_ref,
    ) = more_refs
    columns, count = field_ref.shape
    width = count // parts
    mass = mass_ref[...]
    if weight_before is None:
        field = field_ref[...]
    else:
        field = rim_correction(field_ref[...], left_ref, right_ref, mass, weight_before)
        field_scr[...] = field
    high, low = split_two(field)
    for h in range(parts):
        high_ref[h * columns : (h + 1) * columns] = high[:, h * width : (h + 1) * width]
        low_ref[h * columns : (h + 1) * columns] = low[:, h * width : (h + 1) * width]
    mat_high, mat_low = split_two(matrix_ref[...])
    matrix = jnp.concatenate(
        [
            jnp.concatenate([mat_high, mat_low], axis=1),
            jnp.concatenate([mat_high, jnp.zeros_like(mat_low)], axis=1),
        ],
        axis=0,
    )
    elements = keys_ref.shape[0]
    for start in range(0, elements, group):
        slot = (start // group) % 2
        hot = hot_ref.at[slot]
        found = found_ref.at[slot]
        for e in range(group):
            key = keys_ref[start + e : start + e + 1, :]
            hot[:, e * LANES : (e + 1) * LANES] = one_hot_rows(low_part(key, width), width)
        found[...] = dot(high_ref[...], hot[...]) + dot(low_ref[...], hot[...])
        for e in range(group):
            key = keys_ref[start + e : start + e + 1, :]
            got = pick_part(found[:, e * LANES : (e + 1) * LANES], high_part(key, width), parts)
            got_high, got_low = split_two(got)
            local_ref[e * columns : (e + 1) * columns, :LANES] = got_high
            local_ref[e * columns : (e + 1) * columns, LANES:] = got_low
        product = dot(local_ref[...], matrix)
        for e in range(group):
            key = keys_ref[start + e : start + e + 1, :]
            part = high_part(key, width)
            rows = product[e * columns : (e + 1) * columns]
            value = (rows[:, :LANES] + rows[:, LANES:]) * coef_ref[start + e]
            value_high, value_low = split_two(value)
            for h in range(parts):
                mask = jnp.where(part == h, 1.0, 0.0).astype(BF16)
                span = slice(e * LANES, (e + 1) * LANES)
                yhigh_ref[h * columns : (h + 1) * columns, span] = value_high * mask
                ylow_ref[h * columns : (h + 1) * columns, span] = value_low * mask
        added = dot_nt(yhigh_ref[...], hot[...]) + dot_nt(ylow_ref[...], hot[...])
        if start == 0:
            sum_ref[...] = added
        else:
            sum_ref[...] += added
    for h in range(parts):
        span = slice(h * width, (h + 1) * width)
        before = field_ref[:, span] if weight_before is None else field_scr[:, span]
        stiff = sum_ref[h * columns : (h + 1) * columns]
        out_ref[:, span] = (1.0 - weight) * before + weight * (
            rhs_ref[:, span] - stiff
        ) / mass[:, span]


def loads_kernel(
    parts, brow, weight, nodes_ref, loads_ref, forcing_ref, field_ref, left_ref, right_ref, mass_ref,
    rhs_ref, out_ref, rim_low_ref, rim_high_ref,
):
    nodes = nodes_ref[0:1, :]
    received = loads_ref[...].astype(F32)
    columns, count = field_ref.shape
    span = received.shape[0] // brow
    rows = []
    for r in range(brow):
        piece = received[r * span : (r + 1) * span]
        rows += [piece[:, :columns], piece[:, columns : HALVES * columns]]
    added = scatter_nodes(jnp.transpose(jnp.concatenate(rows, axis=0)), nodes, parts, count)
    rhs_ref[...] = forcing_ref[...] + added
    mass = mass_ref[...]
    field = field_ref[...] + weight * added / mass
    field = rim_correction(field, left_ref, right_ref, mass, weight)
    out_ref[...] = field
    rim_low_ref[...] = field[:, :RIM].astype(BF16)
    rim_high_ref[...] = field[:, count - RIM :].astype(BF16)


def finish_kernel(
    parts, brow, bcol, weight, nodes_ref, field_ref, left_ref, right_ref, mass_ref,
    out_ref, trace_ref, rim_low_ref, rim_high_ref,
):
    field = rim_correction(field_ref[...], left_ref, right_ref, mass_ref[...], weight)
    count = field.shape[1]
    out_ref[...] = field
    rim_low_ref[...] = field[:, :RIM].astype(BF16)
    rim_high_ref[...] = field[:, count - RIM :].astype(BF16)
    write_traces(trace_rows(field, nodes_ref[0:1, :], parts, brow), trace_ref, bcol)


def rim_kernel(
    weight, low_ref, high_ref, left_ref, right_ref, mass_low_ref, mass_high_ref, rim_low_ref, rim_high_ref
):
    step = weight * penalty
    rim_low_ref[...] = (low_ref[...] + step * left_ref[...].astype(F32) / mass_low_ref[...]).astype(BF16)
    rim_high_ref[...] = (
        high_ref[...] + step * right_ref[...].astype(F32) / mass_high_ref[...]
    ).astype(BF16)


def last_kernel(weight, field_ref, left_ref, right_ref, mass_ref, out_ref):
    out_ref[...] = rim_correction(field_ref[...], left_ref, right_ref, mass_ref[...], weight)


def tile_kernel(count_all, source_ref, target_ref, real_ref, imag_ref):
    soften = 0.5 * float(count_all) ** (-1.0 / 3.0)
    rows, cols = real_ref.shape
    step = 16
    for top in range(0, rows, step):
        squared = soften * soften
        for axis in range(3):
            delta = source_ref[top : top + step, axis : axis + 1] - target_ref[axis : axis + 1, :]
            squared = squared + delta * delta
        inverse = lax.rsqrt(squared)
        turns = (squared * inverse) * (wave_number / (2.0 * math.pi))
        turns = turns - jnp.floor(turns + 0.5)
        z = turns * turns
        sine = jnp.full_like(z, SIN_POLY[-1])
        for factor in SIN_POLY[-2::-1]:
            sine = sine * z + factor
        sine = sine * turns
        cosine = jnp.full_like(z, COS_POLY[-1])
        for factor in COS_POLY[-2::-1]:
            cosine = cosine * z + factor
        double = sine * (inverse * (2.0 / math.sqrt(float(count_all))))
        real_ref[top : top + step] = (
            inverse * (1.0 / math.sqrt(float(count_all))) - sine * double
        ).astype(BF16)
        imag_ref[top : top + step] = (cosine * double).astype(BF16)


def potential_kernel(pair, panel_dev, brow, map_ref, trace_ref, real_ref, imag_ref, out_ref, sum_ref):
    step = pl.program_id(0)
    owner, slot = map_ref[0:1, :], map_ref[1:2, :]
    panels = owner.shape[1]
    lane = lax.broadcasted_iota(jnp.int32, (1, panels), 1)
    inside = jnp.where(lane < panel_dev, 0, SLOT_ROWS)
    rows_each = pair * SLOT_ROWS
    key = owner * rows_each + inside + low_part(slot, SLOT_ROWS)
    half = high_part(slot, SLOT_ROWS)
    devices = trace_ref.shape[0]
    rows = trace_ref[...].astype(F32).reshape(devices * rows_each, LANES)
    turned_rows = jnp.transpose(rows).astype(BF16)
    found = dot(turned_rows, one_hot_rows(key, devices * rows_each))
    columns = LANES // HALVES
    density = jnp.where(half == 0, found[:columns], found[columns:])
    turned = jnp.concatenate([-density[columns // 2 :], density[: columns // 2]], axis=0)
    part = dot(density.astype(BF16), real_ref[...]) + dot(turned.astype(BF16), imag_ref[...])

    @pl.when(step == 0)
    def first():
        sum_ref[...] = part

    @pl.when(step > 0)
    def later():
        sum_ref[...] += part

    @pl.when(step == pl.num_programs(0) - 1)
    def write():
        for r in range(brow):
            out_ref[r] = sum_ref[:, r * panel_dev : (r + 1) * panel_dev]


def total(parts_ref):
    value = parts_ref[0]
    for r in range(1, parts_ref.shape[0]):
        value = value + parts_ref[r]
    return value


def send_loads_kernel(devices, own_ref, parts_ref, loads_ref):
    loads_ref[...] = load_rows(total(parts_ref), own_ref[...], devices).astype(BF16)


def sum_kernel(parts_ref, out_ref):
    out_ref[...] = total(parts_ref)


def exchange(rim_low, rim_high):
    count = lax.axis_size("brow") * lax.axis_size("bcol")
    forward = [(i, i + 1) for i in range(count - 1)]
    backward = [(target, source) for source, target in forward]
    low = lax.ppermute(rim_high, AXES, forward)
    high = lax.ppermute(rim_low, AXES, backward)
    return low, high


def swap_all(blocks):
    return lax.all_to_all(blocks, AXES, split_axis=0, concat_axis=0, tiled=True)


def per_device(
    panel_points,
    panel_map,
    element_nodes,
    element_coef,
    element_matrix,
    node_mass,
    forcing,
    field_start,
    potential_start,
):
    columns, panel_dev = potential_start.shape
    count = field_start.shape[1]
    brow, bcol = lax.axis_size("brow"), lax.axis_size("bcol")
    devices = brow * bcol
    count_all = panel_dev * devices
    capacity = max(2, 2 * panel_dev // devices)
    assert capacity <= HALVES * SLOT_ROWS and columns * HALVES == LANES
    parts = 256 // columns
    width = count // parts
    row_panels = bcol * panel_dev
    row_index, col_index = lax.axis_index("brow"), lax.axis_index("bcol")
    self_rank = row_index * bcol + col_index
    slots = HALVES * devices * SLOT_ROWS
    own_map = lax.dynamic_slice_in_dim(panel_map, self_rank * panel_dev, panel_dev, 1)
    row_map = lax.dynamic_slice_in_dim(panel_map, row_index * row_panels, row_panels, 1)
    point_rows = -(-panel_dev // LANES)
    assert 3 * point_rows <= 8
    points = jnp.pad(panel_points, ((0, 0), (0, point_rows * LANES - panel_dev)))
    points = points.reshape(3 * point_rows, LANES)
    points = jnp.pad(points, ((0, 8 - 3 * point_rows), (0, 0)))
    mass = node_mass.reshape(1, count)
    nodes_each, elements = element_nodes.shape
    keys = jnp.pad(element_nodes.T, ((0, 0), (0, LANES - nodes_each)))
    matrix = jnp.pad(element_matrix, ((0, LANES - nodes_each), (0, LANES - nodes_each)))
    smem = pl.BlockSpec(memory_space=pltpu.SMEM)
    vmem = pl.BlockSpec(memory_space=pltpu.VMEM)
    rim_shape = shape_of((columns, RIM), BF16)
    trace_shape = shape_of((devices, bcol * SLOT_ROWS, LANES), BF16)
    field_shape = shape_of((columns, count), F32)

    nodes, small, traces, *rim = call(
        functools.partial(setup_kernel, parts, brow, bcol, panel_dev),
        (shape_of((8, slots), jnp.int32), shape_of((devices, 16, LANES), BF16), trace_shape, rim_shape, rim_shape),
        2_000_000_000,
        in_specs=[smem] + [vmem] * 5,
        out_specs=(vmem,) * 5,
    )(self_rank.reshape(1), panel_map, own_map, field_start, potential_start, points)

    group = 8
    assert elements % group == 0

    def sweep(field, rhs, weight, halo=(), weight_before=None):
        rows = parts * columns
        return call(
            functools.partial(sweep_kernel, parts, weight, weight_before, group),
            field_shape,
            4_000_000_000,
            in_specs=[smem] + [vmem] * (5 + len(halo)),
            out_specs=vmem,
            scratch_shapes=[
                pltpu.VMEM((columns, count), F32),
                pltpu.VMEM((rows, width), BF16),
                pltpu.VMEM((rows, width), BF16),
                pltpu.VMEM((2, width, group * LANES), BF16),
                pltpu.VMEM((2, rows, group * LANES), F32),
                pltpu.VMEM((group * columns, 2 * LANES), BF16),
                pltpu.VMEM((rows, group * LANES), BF16),
                pltpu.VMEM((rows, group * LANES), BF16),
                pltpu.VMEM((rows, width), F32),
            ],
        )(element_coef, field, rhs, mass, keys, matrix, *halo)

    def rims(field, halo, weight):
        low = pl.BlockSpec((columns, RIM), lambda i: (0, 0))
        high = pl.BlockSpec((columns, RIM), lambda i: (0, count // RIM - 1))
        mass_low = pl.BlockSpec((1, RIM), lambda i: (0, 0))
        mass_high = pl.BlockSpec((1, RIM), lambda i: (0, count // RIM - 1))
        whole = pl.BlockSpec((columns, RIM), lambda i: (0, 0))
        return call(
            functools.partial(rim_kernel, weight),
            (rim_shape, rim_shape),
            100_000_000,
            grid=(1,),
            in_specs=[low, high, whole, whole, mass_low, mass_high],
            out_specs=(whole, whole),
        )(field, field, *halo, mass, mass)

    def add_loads(loads, field, halo, weight):
        return call(
            functools.partial(loads_kernel, parts, brow, weight),
            (field_shape, field_shape, rim_shape, rim_shape),
            500_000_000,
            in_specs=[vmem] * 7,
            out_specs=(vmem,) * 4,
        )(nodes, loads, forcing, field, *halo, mass)

    def potential_parts(traces_in, real_tile, imag_tile):
        pair = 2
        rows = pair * panel_dev
        return call(
            functools.partial(potential_kernel, pair, panel_dev, brow),
            shape_of((brow, columns, panel_dev), F32),
            2_000_000_000,
            grid=(bcol // pair,),
            in_specs=[
                pl.BlockSpec((3, rows), lambda i: (0, i)),
                pl.BlockSpec((devices, pair * SLOT_ROWS, LANES), lambda i: (0, i, 0)),
                pl.BlockSpec((rows, brow * panel_dev), lambda i: (i, 0)),
                pl.BlockSpec((rows, brow * panel_dev), lambda i: (i, 0)),
            ],
            out_specs=pl.BlockSpec((brow, columns, panel_dev), lambda i: (0, 0, 0)),
            scratch_shapes=[pltpu.VMEM((columns, brow * panel_dev), F32)],
        )(row_map, traces_in, real_tile, imag_tile)

    weights = [weight_of(sweep_index) for sweep_index in range(SWEEPS)]

    halo = exchange(*rim)
    small_in = swap_all(small)
    traces_in = swap_all(traces)
    field = sweep(field_start, forcing, weights[0])
    loads_in = small_in[:, :SLOT_ROWS].reshape(devices * SLOT_ROWS, LANES)
    all_points = small_in[:, SLOT_ROWS : SLOT_ROWS + 3 * point_rows].astype(F32)
    all_points = all_points.reshape(brow, bcol, 3, point_rows * LANES)[..., :panel_dev]
    source_points = lax.dynamic_index_in_dim(all_points, row_index, 0, keepdims=False)
    source_points = source_points.transpose(0, 2, 1).reshape(row_panels, 3)
    target_points = lax.dynamic_index_in_dim(all_points, col_index, 1, keepdims=False)
    target_points = target_points.transpose(1, 0, 2).reshape(3, brow * panel_dev)
    tile_rows = row_panels // bcol
    tile_shape = shape_of((row_panels, brow * panel_dev), BF16)
    tile_spec = pl.BlockSpec((tile_rows, brow * panel_dev), lambda i: (i, 0))
    real_tile, imag_tile = call(
        functools.partial(tile_kernel, count_all),
        (tile_shape, tile_shape),
        8_000_000_000,
        grid=(bcol,),
        in_specs=[
            pl.BlockSpec((tile_rows, 3), lambda i: (i, 0)),
            pl.BlockSpec((3, brow * panel_dev), lambda i: (0, 0)),
        ],
        out_specs=(tile_spec, tile_spec),
    )(source_points, target_points)
    rhs, field, *rim = add_loads(loads_in, field, halo, weights[0])
    halo = exchange(*rim)
    field = sweep(field, rhs, weights[1])
    parts_out = lax.all_to_all(
        potential_parts(traces_in, real_tile, imag_tile), "brow", split_axis=0, concat_axis=0, tiled=True
    )
    halo_now = exchange(*rims(field, halo, weights[1]))
    field = sweep(field, rhs, weights[2], halo, weights[1])
    loads_out = call(
        functools.partial(send_loads_kernel, devices),
        shape_of((devices * SLOT_ROWS, LANES), BF16),
        100_000_000,
        in_specs=[vmem, vmem],
        out_specs=vmem,
    )(own_map, parts_out)
    loads_in = swap_all(loads_out.reshape(devices, SLOT_ROWS, LANES)).reshape(
        devices * SLOT_ROWS, LANES
    )
    field, traces, *rim = call(
        functools.partial(finish_kernel, parts, brow, bcol, weights[2]),
        (field_shape, trace_shape, rim_shape, rim_shape),
        500_000_000,
        in_specs=[vmem] * 5,
        out_specs=(vmem,) * 4,
    )(nodes, field, *halo_now, mass)

    traces_in = swap_all(traces)
    halo = exchange(*rim)
    field = sweep(field, forcing, weights[0])
    rhs, field, *rim = add_loads(loads_in, field, halo, weights[0])
    halo = exchange(*rim)
    field = sweep(field, rhs, weights[1])
    halo_now = exchange(*rims(field, halo, weights[1]))
    parts_out = lax.all_to_all(
        potential_parts(traces_in, real_tile, imag_tile), "brow", split_axis=0, concat_axis=0, tiled=True
    )
    field = sweep(field, rhs, weights[2], halo, weights[1])
    field = call(
        functools.partial(last_kernel, weights[2]),
        field_shape,
        100_000_000,
        in_specs=[vmem] * 4,
        out_specs=vmem,
    )(field, *halo_now, mass)
    potential = call(
        sum_kernel, shape_of((columns, panel_dev), F32), 1_000_000, in_specs=[vmem], out_specs=vmem
    )(parts_out)
    return (field, potential)


def solution(mesh):
    placed = (
        P(None, AXES),
        P(),
        P(None, AXES),
        P(AXES),
        P(),
        P(AXES),
        P(None, AXES),
        P(None, AXES),
        P(None, AXES),
    )
    return jax.shard_map(
        per_device,
        mesh=mesh,
        in_specs=placed,
        out_specs=(P(None, AXES), P(None, AXES)),
        check_vma=False,
    )
```

time: 599 us -> 200 us (0.33); the launches traced: 589 us -> 196 us
  other arithmetic: 203 us -> 0.01 us
  local copies, waits for them, and re-layouts: 187 us -> 16.9 us
  Pallas kernels: 0 us -> 90.5 us
  blocking collectives: 49.4 us -> 0 us
  waiting for transfers between devices: 35.1 us -> 0.05 us
  matrix products: 26.2 us -> 0 us
  starting transfers between devices: 70.5 us -> 87.7 us
  between operations: 15.4 us -> 1.12 us
    scatter-add x20 -> x0, other arithmetic: 155 us -> none  [the longest x6 139 us: apply_operator(): jnp.zeros_like(field_now).at[:, element_nodes].add(stiffness)]
    gather x16 -> x0, local copies, waits for them, and re-layouts: 111 us -> none  [the longest x12 107 us: apply_operator(): gathered = jnp.take(field_now, element_nodes, axis=1)]
    pallas_call x0 -> x18, Pallas kernels: none -> 90.5 us  [the longest x6 51.2 us: sweep(): call(functools.partial(sweep_kernel, parts, weight, weight_before, group)...]
    all_gather x4 -> x0, blocking collectives: 49.4 us -> none  [the longest x2 28.6 us: per_device(): lax.all_gather(densities, 'bcol', axis=1, tiled=True)]
    unnamed x4 -> x0, waiting for transfers between devices: 35.1 us -> none
    dot_general x14 -> x0, matrix products: 26.2 us -> none  [the longest x6 18.2 us: apply_operator(): jnp.einsum('jk,cke->cje', element_matrix, gathered, precision=lax.Precisi...]
    scatter x3 -> x0, local copies, waits for them, and re-layouts: 25.2 us -> none  [the longest x1 23 us: per_device(): jnp.zeros((slot_total,), jnp.int32).at[table_index]]
    mul x6 -> x0, local copies, waits for them, and re-layouts: 23 us -> none  [apply_operator(): jnp.einsum('jk,cke->cje', element_matrix, gathered, precision=lax.Precisi...]
  transfers between devices with their start and end apart: 18 -> 18, of which waited for: 2 -> 0; matrix products, arithmetic and copies ran while one was open for 50% -> 3% of each run, Pallas kernels for 0% -> 44%
where the time goes in v1:
time: 200 us; the launch traced here: 196 us
  Pallas kernels  90.5 us (45%)
  starting transfers between devices  87.7 us (44%)
  local copies, waits for them, and re-layouts  16.9 us (8%)
    pallas_call x6, Pallas kernels, sweep(): call(functools.partial(sweep_kernel, parts, weight, weight_before, group)...  51.2 us
    ppermute x6, starting transfers between devices, exchange(): high = lax.ppermute(rim_low, AXES, backward)  43.2 us
    all_to_all x4, starting transfers between devices, swap_all(): return lax.all_to_all(blocks, AXES, split_axis=0, concat_axis=0, tiled=True)  25.8 us
    ppermute x6, starting transfers between devices, exchange(): low = lax.ppermute(rim_high, AXES, forward)  11.7 us
    pallas_call x2, Pallas kernels, potential_parts(): call(functools.partial(potential_kernel, pair, panel_dev, brow), shape_of...  11 us
    pallas_call x1, Pallas kernels, per_device(): call(functools.partial(tile_kernel, count_all), (tile_shape, tile_shape),...  9.18 us
    unnamed x38, local copies, waits for them, and re-layouts  9.01 us
    all_to_all x2, starting transfers between devices, per_device(): lax.all_to_all(potential_parts(traces_in, real_tile, imag_tile), 'brow',...  7.04 us
  transfers between devices with their start and end apart: 18, of which 0 were waited for; matrix products, arithmetic and copies ran while one was open for 3% of the time, Pallas kernels for 44%

profile of v1, /device:TPU:4, one launch (start us, length us, event | category | flops | bytes accessed | tf_op | source)
XLA Modules:
  0.0 196.2 jit_solution(3423524979978355244)
XLA Ops:
  0.6 0.7 pad.16
  1.3 0.6 pad.17.points_ref
  1.9 1.4 constant_dynamic-slice_fusion.3.own_ref
  3.3 3.0 %shard_map.104 = (s32[8,512]{1,0:T(8,128)}, bf16[32,16,128]{2,1,0:T(8,128)(2,1)}, bf16[32,64,128]{2,1,0:T(8,128)(2,1)}, bf16[64,128]{1,0:T(8,128)(2,1)}, bf16[64,128]{1,0:T(8,128)(2,1)}) custom-call(s32[1]{0:T(128)} %bitcast.rank_ref, s32[3,6144]{1,0:T(4,128)} %map_ref.1, s32[3,192]{1,0:T(4,128)} %constant_dynamic-slice_fusion.3.own_ref, ...), custom_call_target="tpu_custom_call" | custom-call | flops 2000000000 | bytes 1048576 | tf_op jit(solution)/shard_map/pallas_call | solution.py:424
  6.3 6.1 %all-to-all-start.1 = ((bf16[32,16,128]{2,1,0:T(8,128)(2,1)}), bf16[32,16,128]{2,1,0:T(8,128)(2,1)S(1)}, u32[]{:S(2)}, u32[]{:S(2)}) async-start(bf16[32,16,128]{2,1,0:T(8,128)(2,1)} %get-tuple-element.27), calls=%async_computation.1 | async-start | bytes 262144 | tf_op jit(solution)/shard_map/all_to_all | solution.py:380
  12.4 2.1 %collective-permute-start = (bf16[64,128]{1,0:T(8,128)(2,1)}, bf16[64,128]{1,0:T(8,128)(2,1)S(1)}, u32[]{:S(2)}, u32[]{:S(2)}) collective-permute-start(bf16[64,128]{1,0:T(8,128)(2,1)} %get-tuple-element.30), channel_id=1, source_target_pairs={{0,1},{1,2},{2,3},{3,4},{4,5},{5,6},{6,7},{7,8},{8,9},{9,10},{10,1... | collective-permute-start | bytes 49160 | tf_op jit(solution)/shard_map/ppermute | solution.py:374
  14.5 7.1 %collective-permute-start.1 = (bf16[64,128]{1,0:T(8,128)(2,1)}, bf16[64,128]{1,0:T(8,128)(2,1)S(1)}, u32[]{:S(2)}, u32[]{:S(2)}) collective-permute-start(bf16[64,128]{1,0:T(8,128)(2,1)} %get-tuple-element.31), channel_id=1, source_target_pairs={{1,0},{2,1},{3,2},{4,3},{5,4},{6,5},{7,6},{8,7},{9,8},{10,9},{11,1... | collective-permute-start | bytes 49160 | tf_op jit(solution)/shard_map/ppermute | solution.py:375
  21.6 0.6 pad.18.keys_ref
  22.2 0.6 pad.19.matrix_ref
  22.9 8.5 %shard_map.108.field_ref = f32[64,2048]{1,0:T(8,128)} custom-call(f32[32]{0:T(128)} %coef_ref.11, f32[64,2048]{1,0:T(8,128)} %field_ref.3, f32[64,2048]{1,0:T(8,128)} %forcing_ref.3, f32[1,2048]{1,0:T(1,128)} %bitcast.18, s32[32,128]{1,0:T(8,128)} %pad.18.keys_ref, f32[128,128]{1,0:T(8,128)} %pad.19.matrix_ref), custom_call_target="tpu_custom_call" | custom-call | flops 4000000000 | bytes 1048576 | tf_op jit(solution)/shard_map/pallas_call | solution.py:437
  31.4 1.3 constant_dynamic-slice_fusion.2.map_ref
  32.7 2.3 %all-to-all-start = ((bf16[32,64,128]{2,1,0:T(8,128)(2,1)}), bf16[32,64,128]{2,1,0:T(8,128)(2,1)S(1)}, u32[]{:S(2)}, u32[]{:S(2)}) async-start(bf16[32,64,128]{2,1,0:T(8,128)(2,1)} %get-tuple-element.26), calls=%async_computation | async-start | bytes 1048576 | tf_op jit(solution)/shard_map/all_to_all | solution.py:380
  35.1 0.1 reshape.34
  35.2 0.6 slice_bitcast_fusion.loads_ref
  35.8 1.2 copy.16
  37.1 0.7 reshape.36.target_ref
  37.8 0.0 collective-permute-done.1.right_ref
  37.8 0.6 copy-done.13
  38.4 0.0 copy-done.14
  38.4 2.7 %shard_map.109 = (f32[64,2048]{1,0:T(8,128)}, f32[64,2048]{1,0:T(8,128)}, bf16[64,128]{1,0:T(8,128)(2,1)}, bf16[64,128]{1,0:T(8,128)(2,1)}) custom-call(s32[8,512]{1,0:T(8,128)} %get-tuple-element.25.nodes_ref, bf16[256,128]{1,0:T(8,128)(2,1)} %slice_bitcast_fusion.loads_ref, f32[64,2048]{1,0:T(8,128)} %forcing_ref.3, f32[64,2048]{1,0:T(8,128)} %shard_map.108.field_ref, ...), custom_call_target="tpu_custom_call" | custom-call | flops 500000000 | bytes 1048576 | tf_op jit(solution)/shard_map/pallas_call | solution.py:472
  41.1 1.9 collective-permute-start.2
  43.0 7.2 %collective-permute-start.3 = (bf16[64,128]{1,0:T(8,128)(2,1)}, bf16[64,128]{1,0:T(8,128)(2,1)S(1)}, u32[]{:S(2)}, u32[]{:S(2)}) collective-permute-start(bf16[64,128]{1,0:T(8,128)(2,1)} %get-tuple-element.35), channel_id=1, source_target_pairs={{1,0},{2,1},{3,2},{4,3},{5,4},{6,5},{7,6},{8,7},{9,8},{10,9},{11,1... | collective-permute-start | bytes 49160 | tf_op jit(solution)/shard_map/ppermute | solution.py:375
  50.2 9.2 %shard_map.105 = (bf16[1536,768]{1,0:T(8,128)(2,1)}, bf16[1536,768]{1,0:T(8,128)(2,1)}) custom-call(f32[1536,3]{1,0:T(8,128)} %bitcast.17, f32[3,768]{1,0:T(4,128)} %reshape.36.target_ref), custom_call_target="tpu_custom_call" | custom-call | flops 8000000000 | bytes 1048576 | tf_op jit(solution)/shard_map/pallas_call | solution.py:514
  59.4 0.8 copy-done.1
  60.2 5.5 %shard_map.106 = f32[4,64,192]{2,1,0:T(8,128)} custom-call(s32[3,1536]{1,0:T(4,128)} %constant_dynamic-slice_fusion.2.map_ref, bf16[32,64,128]{2,1,0:T(8,128)(2,1)} %copy-done.1, bf16[1536,768]{1,0:T(8,128)(2,1)} %get-tuple-element.28.real_ref, bf16[1536,768]{1,0:T(8,128)(2,1)} %get-tuple-element.29.imag_ref), custom_call_target="tpu_custom_call" | custom-call | flops 2000000000 | bytes 1048576 | tf_op jit(solution)/shard_map/pallas_call | solution.py:483
  65.7 3.7 %all-to-all-start.2 = ((f32[4,64,192]{2,1,0:T(8,128)}), f32[4,64,192]{2,1,0:T(8,128)S(1)}, u32[]{:S(2)}, u32[]{:S(2)}) async-start(f32[4,64,192]{2,1,0:T(8,128)} %shard_map.106), calls=%async_computation.2 | async-start | bytes 524288 | tf_op jit(solution)/shard_map/all_to_all | solution.py:528
  69.4 8.5 %shard_map.110.field_ref.low_ref.high_ref = f32[64,2048]{1,0:T(8,128)} custom-call(f32[32]{0:T(128)} %coef_ref.11, f32[64,2048]{1,0:T(8,128)} %get-tuple-element.32.field_ref, f32[64,2048]{1,0:T(8,128)} %get-tuple-element.33.rhs_ref, f32[1,2048]{1,0:T(1,128)} %bitcast.20, s32[32,128]{1,0:T(8,128)} %pad.18.keys_ref, f32[128,128]{1,0:T(8,128)} %pad.19.matrix_ref), custom_call_target="tpu_custom_call" | custom-call | flops 4000000000 | bytes 1048576 | tf_op jit(solution)/shard_map/pallas_call | solution.py:437
  77.9 0.6 copy-done.6
  78.5 0.6 copy-done.7
  79.1 1.4 shard_map.112
  80.5 1.9 collective-permute-start.4
  82.4 7.2 %collective-permute-start.5 = (bf16[64,128]{1,0:T(8,128)(2,1)}, bf16[64,128]{1,0:T(8,128)(2,1)S(1)}, u32[]{:S(2)}, u32[]{:S(2)}) collective-permute-start(bf16[64,128]{1,0:T(8,128)(2,1)} %get-tuple-element.37), channel_id=1, source_target_pairs={{1,0},{2,1},{3,2},{4,3},{5,4},{6,5},{7,6},{8,7},{9,8},{10,9},{11,1... | collective-permute-start | bytes 49160 | tf_op jit(solution)/shard_map/ppermute | solution.py:375
  89.7 0.7 copy-done.3
  90.4 1.9 shard_map.107
  92.3 2.3 %all-to-all-start.3 = ((bf16[32,8,128]{2,1,0:T(8,128)(2,1)}), bf16[32,8,128]{2,1,0:T(8,128)(2,1)S(1)}, u32[]{:S(2)}, u32[]{:S(2)}) async-start(bf16[32,8,128]{2,1,0:T(8,128)(2,1)} %bitcast.33), calls=%async_computation.3 | async-start | bytes 131072 | tf_op jit(solution)/shard_map/all_to_all | solution.py:380
  94.6 8.6 %shard_map.111.field_ref = f32[64,2048]{1,0:T(8,128)} custom-call(f32[32]{0:T(128)} %coef_ref.11, f32[64,2048]{1,0:T(8,128)} %shard_map.110.field_ref.low_ref.high_ref, f32[64,2048]{1,0:T(8,128)} %get-tuple-element.33.rhs_ref, f32[1,2048]{1,0:T(1,128)} %bitcast.23, s32[32,128]{1,0:T(8,128)} %pad.18.keys_ref, f32[128,128]{1,0:T(8,128)} %pad.19.matrix_ref, ...), custom_call_target="tpu_custom_call" | custom-call | flops 4000000000 | bytes 1048576 | tf_op jit(solution)/shard_map/pallas_call | solution.py:437
  103.2 0.6 copy-done.15
  103.8 0.6 copy-done.16
  104.4 2.4 %shard_map.113 = (f32[64,2048]{1,0:T(8,128)}, bf16[32,64,128]{2,1,0:T(8,128)(2,1)}, bf16[64,128]{1,0:T(8,128)(2,1)}, bf16[64,128]{1,0:T(8,128)(2,1)}) custom-call(s32[8,512]{1,0:T(8,128)} %get-tuple-element.25.nodes_ref, f32[64,2048]{1,0:T(8,128)} %shard_map.111.field_ref, bf16[64,128]{1,0:T(8,128)(2,1)} %copy-done.15, bf16[64,128]{1,0:T(8,128)(2,1)} %copy-done.16, ...), custom_call_target="tpu_custom_call" | custom-call | flops 500000000 | bytes 1048576 | tf_op jit(solution)/shard_map/pallas_call | solution.py:543
  106.8 15.0 %all-to-all-start.4 = ((bf16[32,64,128]{2,1,0:T(8,128)(2,1)}), bf16[32,64,128]{2,1,0:T(8,128)(2,1)S(1)}, u32[]{:S(2)}, u32[]{:S(2)}) async-start(bf16[32,64,128]{2,1,0:T(8,128)(2,1)} %get-tuple-element.47), calls=%async_computation.4 | async-start | bytes 1048576 | tf_op jit(solution)/shard_map/all_to_all | solution.py:380
  121.8 2.0 %collective-permute-start.6 = (bf16[64,128]{1,0:T(8,128)(2,1)}, bf16[64,128]{1,0:T(8,128)(2,1)S(1)}, u32[]{:S(2)}, u32[]{:S(2)}) collective-permute-start(bf16[64,128]{1,0:T(8,128)(2,1)} %get-tuple-element.39), channel_id=1, source_target_pairs={{0,1},{1,2},{2,3},{3,4},{4,5},{5,6},{6,7},{7,8},{8,9},{9,10},{10,1... | collective-permute-start | bytes 49160 | tf_op jit(solution)/shard_map/ppermute | solution.py:374
  123.9 7.1 %collective-permute-start.7 = (bf16[64,128]{1,0:T(8,128)(2,1)}, bf16[64,128]{1,0:T(8,128)(2,1)S(1)}, u32[]{:S(2)}, u32[]{:S(2)}) collective-permute-start(bf16[64,128]{1,0:T(8,128)(2,1)} %get-tuple-element.40), channel_id=1, source_target_pairs={{1,0},{2,1},{3,2},{4,3},{5,4},{6,5},{7,6},{8,7},{9,8},{10,9},{11,1... | collective-permute-start | bytes 49160 | tf_op jit(solution)/shard_map/ppermute | solution.py:375
  131.0 8.5 %shard_map.114.field_ref = f32[64,2048]{1,0:T(8,128)} custom-call(f32[32]{0:T(128)} %coef_ref.11, f32[64,2048]{1,0:T(8,128)} %get-tuple-element.38.field_ref, f32[64,2048]{1,0:T(8,128)} %forcing_ref.3, f32[1,2048]{1,0:T(1,128)} %bitcast.25, s32[32,128]{1,0:T(8,128)} %pad.18.keys_ref, f32[128,128]{1,0:T(8,128)} %pad.19.matrix_ref), custom_call_target="tpu_custom_call" | custom-call | flops 4000000000 | bytes 1048576 | tf_op jit(solution)/shard_map/pallas_call | solution.py:437
  139.6 0.6 copy-done.17
  140.1 0.0 copy-done.18
  140.2 2.7 %shard_map.115 = (f32[64,2048]{1,0:T(8,128)}, f32[64,2048]{1,0:T(8,128)}, bf16[64,128]{1,0:T(8,128)(2,1)}, bf16[64,128]{1,0:T(8,128)(2,1)}) custom-call(s32[8,512]{1,0:T(8,128)} %get-tuple-element.25.nodes_ref, bf16[256,128]{1,0:T(8,128)(2,1)} %bitcast.32, f32[64,2048]{1,0:T(8,128)} %forcing_ref.3, f32[64,2048]{1,0:T(8,128)} %shard_map.114.field_ref, ...), custom_call_target="tpu_custom_call" | custom-call | flops 500000000 | bytes 1048576 | tf_op jit(solution)/shard_map/pallas_call | solution.py:472
  142.8 1.9 collective-permute-start.8
  144.7 7.2 %collective-permute-start.9 = (bf16[64,128]{1,0:T(8,128)(2,1)}, bf16[64,128]{1,0:T(8,128)(2,1)S(1)}, u32[]{:S(2)}, u32[]{:S(2)}) collective-permute-start(bf16[64,128]{1,0:T(8,128)(2,1)} %get-tuple-element.44), channel_id=1, source_target_pairs={{1,0},{2,1},{3,2},{4,3},{5,4},{6,5},{7,6},{8,7},{9,8},{10,9},{11,1... | collective-permute-start | bytes 49160 | tf_op jit(solution)/shard_map/ppermute | solution.py:375
  152.0 8.5 %shard_map.116.field_ref.low_ref.high_ref = f32[64,2048]{1,0:T(8,128)} custom-call(f32[32]{0:T(128)} %coef_ref.11, f32[64,2048]{1,0:T(8,128)} %get-tuple-element.41.field_ref, f32[64,2048]{1,0:T(8,128)} %get-tuple-element.42.rhs_ref, f32[1,2048]{1,0:T(1,128)} %bitcast.27, s32[32,128]{1,0:T(8,128)} %pad.18.keys_ref, f32[128,128]{1,0:T(8,128)} %pad.19.matrix_ref), custom_call_target="tpu_custom_call" | custom-call | flops 4000000000 | bytes 1048576 | tf_op jit(solution)/shard_map/pallas_call | solution.py:437
  160.5 0.8 copy-done.2
  161.4 5.5 %shard_map.120 = f32[4,64,192]{2,1,0:T(8,128)} custom-call(s32[3,1536]{1,0:T(4,128)} %constant_dynamic-slice_fusion.2.map_ref, bf16[32,64,128]{2,1,0:T(8,128)(2,1)} %copy-done.2, bf16[1536,768]{1,0:T(8,128)(2,1)} %get-tuple-element.28.real_ref, bf16[1536,768]{1,0:T(8,128)(2,1)} %get-tuple-element.29.imag_ref), custom_call_target="tpu_custom_call" | custom-call | flops 2000000000 | bytes 1048576 | tf_op jit(solution)/shard_map/pallas_call | solution.py:483
  166.9 3.4 %all-to-all-start.5 = ((f32[4,64,192]{2,1,0:T(8,128)}), f32[4,64,192]{2,1,0:T(8,128)S(1)}, u32[]{:S(2)}, u32[]{:S(2)}) async-start(f32[4,64,192]{2,1,0:T(8,128)} %shard_map.120), calls=%async_computation.5 | async-start | bytes 524288 | tf_op jit(solution)/shard_map/all_to_all | solution.py:558
  170.3 0.0 copy-start.8
  170.3 0.6 copy-done.8
  170.9 0.6 copy-done.9
  171.5 1.4 shard_map.118
  172.9 1.9 collective-permute-start.10
  174.8 7.2 %collective-permute-start.11 = (bf16[64,128]{1,0:T(8,128)(2,1)}, bf16[64,128]{1,0:T(8,128)(2,1)S(1)}, u32[]{:S(2)}, u32[]{:S(2)}) collective-permute-start(bf16[64,128]{1,0:T(8,128)(2,1)} %get-tuple-element.46), channel_id=1, source_target_pairs={{1,0},{2,1},{3,2},{4,3},{5,4},{6,5},{7,6},{8,7},{9,8},{10,9},{11,1... | collective-permute-start | bytes 49160 | tf_op jit(solution)/shard_map/ppermute | solution.py:375
  182.1 8.6 %shard_map.117.field_ref = f32[64,2048]{1,0:T(8,128)} custom-call(f32[32]{0:T(128)} %coef_ref.11, f32[64,2048]{1,0:T(8,128)} %shard_map.116.field_ref.low_ref.high_ref, f32[64,2048]{1,0:T(8,128)} %get-tuple-element.42.rhs_ref, f32[1,2048]{1,0:T(1,128)} %bitcast.30, s32[32,128]{1,0:T(8,128)} %pad.18.keys_ref, f32[128,128]{1,0:T(8,128)} %pad.19.matrix_ref, ...), custom_call_target="tpu_custom_call" | custom-call | flops 4000000000 | bytes 1048576 | tf_op jit(solution)/shard_map/pallas_call | solution.py:437
  190.6 0.6 copy-done.10
  191.2 0.6 copy-done.11
  191.8 1.9 shard_map.119
  193.7 0.7 copy-done
  194.4 1.6 shard_map.121
  (44 shorter events, 0.1 us)
Async XLA Ops:
  3.3 18.3 %copy-start.12 = (s32[125,32]{0,1:T(8,128)S(1)}, s32[125,32]{0,1:T(8,128)}, u32[]{:S(2)}) copy-start(s32[125,32]{0,1:T(8,128)} %param.11) | copy-start | bytes 48004
  3.3 18.9 %copy-start.4 = (f32[125,125]{1,0:T(8,128)S(1)}, f32[125,125]{1,0:T(8,128)}, u32[]{:S(2)}) copy-start(f32[125,125]{1,0:T(8,128)} %param.13) | copy-start | bytes 187504
  6.3 26.4 %all-to-all-start.1 = ((bf16[32,16,128]{2,1,0:T(8,128)(2,1)}), bf16[32,16,128]{2,1,0:T(8,128)(2,1)S(1)}, u32[]{:S(2)}, u32[]{:S(2)}) async-start(bf16[32,16,128]{2,1,0:T(8,128)(2,1)} %get-tuple-element.27), calls=%async_computation.1 | async-start | bytes 262144 | tf_op jit(solution)/shard_map/all_to_all | solution.py:380
  12.4 25.3 %collective-permute-start = (bf16[64,128]{1,0:T(8,128)(2,1)}, bf16[64,128]{1,0:T(8,128)(2,1)S(1)}, u32[]{:S(2)}, u32[]{:S(2)}) collective-permute-start(bf16[64,128]{1,0:T(8,128)(2,1)} %get-tuple-element.30), channel_id=1, source_target_pairs={{0,1},{1,2},{2,3},{3,4},{4,5},{5,6},{6,7},{7,8},{8,9},{9,10},{10,1... | collective-permute-start | bytes 49160 | tf_op jit(solution)/shard_map/ppermute | solution.py:374
  14.5 23.3 %collective-permute-start.1 = (bf16[64,128]{1,0:T(8,128)(2,1)}, bf16[64,128]{1,0:T(8,128)(2,1)S(1)}, u32[]{:S(2)}, u32[]{:S(2)}) collective-permute-start(bf16[64,128]{1,0:T(8,128)(2,1)} %get-tuple-element.31), channel_id=1, source_target_pairs={{1,0},{2,1},{3,2},{4,3},{5,4},{6,5},{7,6},{8,7},{9,8},{10,9},{11,1... | collective-permute-start | bytes 49160 | tf_op jit(solution)/shard_map/ppermute | solution.py:375
  32.7 26.7 %all-to-all-start = ((bf16[32,64,128]{2,1,0:T(8,128)(2,1)}), bf16[32,64,128]{2,1,0:T(8,128)(2,1)S(1)}, u32[]{:S(2)}, u32[]{:S(2)}) async-start(bf16[32,64,128]{2,1,0:T(8,128)(2,1)} %get-tuple-element.26), calls=%async_computation | async-start | bytes 1048576 | tf_op jit(solution)/shard_map/all_to_all | solution.py:380
  37.8 0.6 copy-start.13
  37.8 0.6 copy-start.14
  41.1 36.8 %collective-permute-start.2 = (bf16[64,128]{1,0:T(8,128)(2,1)}, bf16[64,128]{1,0:T(8,128)(2,1)S(1)}, u32[]{:S(2)}, u32[]{:S(2)}) collective-permute-start(bf16[64,128]{1,0:T(8,128)(2,1)} %get-tuple-element.34), channel_id=1, source_target_pairs={{0,1},{1,2},{2,3},{3,4},{4,5},{5,6},{6,7},{7,8},{8,9},{9,10},{10,1... | collective-permute-start | bytes 49160 | tf_op jit(solution)/shard_map/ppermute | solution.py:374
  43.0 34.9 %collective-permute-start.3 = (bf16[64,128]{1,0:T(8,128)(2,1)}, bf16[64,128]{1,0:T(8,128)(2,1)S(1)}, u32[]{:S(2)}, u32[]{:S(2)}) collective-permute-start(bf16[64,128]{1,0:T(8,128)(2,1)} %get-tuple-element.35), channel_id=1, source_target_pairs={{1,0},{2,1},{3,2},{4,3},{5,4},{6,5},{7,6},{8,7},{9,8},{10,9},{11,1... | collective-permute-start | bytes 49160 | tf_op jit(solution)/shard_map/ppermute | solution.py:375
  59.4 0.8 copy-start.1
  65.7 24.0 %all-to-all-start.2 = ((f32[4,64,192]{2,1,0:T(8,128)}), f32[4,64,192]{2,1,0:T(8,128)S(1)}, u32[]{:S(2)}, u32[]{:S(2)}) async-start(f32[4,64,192]{2,1,0:T(8,128)} %shard_map.106), calls=%async_computation.2 | async-start | bytes 524288 | tf_op jit(solution)/shard_map/all_to_all | solution.py:528
  77.9 0.6 copy-start.6
  78.5 0.6 copy-start.7
  80.5 22.7 %collective-permute-start.4 = (bf16[64,128]{1,0:T(8,128)(2,1)}, bf16[64,128]{1,0:T(8,128)(2,1)S(1)}, u32[]{:S(2)}, u32[]{:S(2)}) collective-permute-start(bf16[64,128]{1,0:T(8,128)(2,1)} %get-tuple-element.36), channel_id=1, source_target_pairs={{0,1},{1,2},{2,3},{3,4},{4,5},{5,6},{6,7},{7,8},{8,9},{9,10},{10,1... | collective-permute-start | bytes 49160 | tf_op jit(solution)/shard_map/ppermute | solution.py:374
  82.4 20.8 %collective-permute-start.5 = (bf16[64,128]{1,0:T(8,128)(2,1)}, bf16[64,128]{1,0:T(8,128)(2,1)S(1)}, u32[]{:S(2)}, u32[]{:S(2)}) collective-permute-start(bf16[64,128]{1,0:T(8,128)(2,1)} %get-tuple-element.37), channel_id=1, source_target_pairs={{1,0},{2,1},{3,2},{4,3},{5,4},{6,5},{7,6},{8,7},{9,8},{10,9},{11,1... | collective-permute-start | bytes 49160 | tf_op jit(solution)/shard_map/ppermute | solution.py:375
  89.7 0.7 copy-start.3
  92.3 14.5 %all-to-all-start.3 = ((bf16[32,8,128]{2,1,0:T(8,128)(2,1)}), bf16[32,8,128]{2,1,0:T(8,128)(2,1)S(1)}, u32[]{:S(2)}, u32[]{:S(2)}) async-start(bf16[32,8,128]{2,1,0:T(8,128)(2,1)} %bitcast.33), calls=%async_computation.3 | async-start | bytes 131072 | tf_op jit(solution)/shard_map/all_to_all | solution.py:380
  103.2 0.6 copy-start.15
  103.8 0.6 copy-start.16
  106.8 32.8 %copy-start.5 = (bf16[32,8,128]{2,1,0:T(8,128)(2,1)}, bf16[32,8,128]{2,1,0:T(8,128)(2,1)S(1)}, u32[]{:S(2)}) copy-start(bf16[32,8,128]{2,1,0:T(8,128)(2,1)S(1)} %all-to-all-done.3) | copy-start | bytes 196612
  106.8 53.7 %all-to-all-start.4 = ((bf16[32,64,128]{2,1,0:T(8,128)(2,1)}), bf16[32,64,128]{2,1,0:T(8,128)(2,1)S(1)}, u32[]{:S(2)}, u32[]{:S(2)}) async-start(bf16[32,64,128]{2,1,0:T(8,128)(2,1)} %get-tuple-element.47), calls=%async_computation.4 | async-start | bytes 1048576 | tf_op jit(solution)/shard_map/all_to_all | solution.py:380
  121.8 17.7 %collective-permute-start.6 = (bf16[64,128]{1,0:T(8,128)(2,1)}, bf16[64,128]{1,0:T(8,128)(2,1)S(1)}, u32[]{:S(2)}, u32[]{:S(2)}) collective-permute-start(bf16[64,128]{1,0:T(8,128)(2,1)} %get-tuple-element.39), channel_id=1, source_target_pairs={{0,1},{1,2},{2,3},{3,4},{4,5},{5,6},{6,7},{7,8},{8,9},{9,10},{10,1... | collective-permute-start | bytes 49160 | tf_op jit(solution)/shard_map/ppermute | solution.py:374
  123.9 15.7 %collective-permute-start.7 = (bf16[64,128]{1,0:T(8,128)(2,1)}, bf16[64,128]{1,0:T(8,128)(2,1)S(1)}, u32[]{:S(2)}, u32[]{:S(2)}) collective-permute-start(bf16[64,128]{1,0:T(8,128)(2,1)} %get-tuple-element.40), channel_id=1, source_target_pairs={{1,0},{2,1},{3,2},{4,3},{5,4},{6,5},{7,6},{8,7},{9,8},{10,9},{11,1... | collective-permute-start | bytes 49160 | tf_op jit(solution)/shard_map/ppermute | solution.py:375
  139.5 0.6 copy-start.17
  139.6 0.6 copy-start.18
  142.8 27.4 %collective-permute-start.8 = (bf16[64,128]{1,0:T(8,128)(2,1)}, bf16[64,128]{1,0:T(8,128)(2,1)S(1)}, u32[]{:S(2)}, u32[]{:S(2)}) collective-permute-start(bf16[64,128]{1,0:T(8,128)(2,1)} %get-tuple-element.43), channel_id=1, source_target_pairs={{0,1},{1,2},{2,3},{3,4},{4,5},{5,6},{6,7},{7,8},{8,9},{9,10},{10,1... | collective-permute-start | bytes 49160 | tf_op jit(solution)/shard_map/ppermute | solution.py:374
  144.7 25.5 %collective-permute-start.9 = (bf16[64,128]{1,0:T(8,128)(2,1)}, bf16[64,128]{1,0:T(8,128)(2,1)S(1)}, u32[]{:S(2)}, u32[]{:S(2)}) collective-permute-start(bf16[64,128]{1,0:T(8,128)(2,1)} %get-tuple-element.44), channel_id=1, source_target_pairs={{1,0},{2,1},{3,2},{4,3},{5,4},{6,5},{7,6},{8,7},{9,8},{10,9},{11,1... | collective-permute-start | bytes 49160 | tf_op jit(solution)/shard_map/ppermute | solution.py:375
  160.5 0.8 copy-start.2
  166.9 26.9 %all-to-all-start.5 = ((f32[4,64,192]{2,1,0:T(8,128)}), f32[4,64,192]{2,1,0:T(8,128)S(1)}, u32[]{:S(2)}, u32[]{:S(2)}) async-start(f32[4,64,192]{2,1,0:T(8,128)} %shard_map.120), calls=%async_computation.5 | async-start | bytes 524288 | tf_op jit(solution)/shard_map/all_to_all | solution.py:558
  170.3 0.6 copy-start.8
  170.9 0.6 copy-start.9
  172.9 17.7 %collective-permute-start.10 = (bf16[64,128]{1,0:T(8,128)(2,1)}, bf16[64,128]{1,0:T(8,128)(2,1)S(1)}, u32[]{:S(2)}, u32[]{:S(2)}) collective-permute-start(bf16[64,128]{1,0:T(8,128)(2,1)} %get-tuple-element.45), channel_id=1, source_target_pairs={{0,1},{1,2},{2,3},{3,4},{4,5},{5,6},{6,7},{7,8},{8,9},{9,10},{10,1... | collective-permute-start | bytes 49160 | tf_op jit(solution)/shard_map/ppermute | solution.py:374
  174.8 15.8 %collective-permute-start.11 = (bf16[64,128]{1,0:T(8,128)(2,1)}, bf16[64,128]{1,0:T(8,128)(2,1)S(1)}, u32[]{:S(2)}, u32[]{:S(2)}) collective-permute-start(bf16[64,128]{1,0:T(8,128)(2,1)} %get-tuple-element.46), channel_id=1, source_target_pairs={{1,0},{2,1},{3,2},{4,3},{5,4},{6,5},{7,6},{8,7},{9,8},{10,9},{11,1... | collective-permute-start | bytes 49160 | tf_op jit(solution)/shard_map/ppermute | solution.py:375
  190.6 0.6 copy-start.10
  191.2 0.6 copy-start.11
  193.7 0.7 copy-start
